TPU v7x, 512 devices: a whole 4x8x8 slice. The times are simulated.
512 devices in a mesh: sx: 4 (over y_lo, core), sy: 8 (over z), af: 16 (over y_hi, x).
Axes of the slice: x: 4, y: 8 (y_hi: 4, y_lo: 2; y = y_hi * 2 + y_lo), z: 8, core: 2. Of those that a mesh axis runs over, the one named last changes fastest.
Arguments:
- inputs: bfloat16 [32, 32, 8, 4, 512], P(None, 'af', 'sy', 'sx'), may hold values from -6 to 6
- weight_one: bfloat16 [27, 64, 32], replicated, may hold values from -0.21875 to 0.21875
- weight_two: bfloat16 [27, 128, 64], P(None, 'af'), may hold values from -0.15625 to 0.15625
- cotangent: bfloat16 [128, 16, 8, 4, 128], P(None, 'af', 'sy', 'sx'), may hold values from -6 to 6
Outputs:
- output: bfloat16 [128, 16, 8, 4, 128], P(None, 'af', 'sy', 'sx')
- grad_one: float32 [27, 64, 32], replicated
- grad_two: float32 [27, 128, 64], P(None, 'af')
All inputs are finite; a program needn't handle non-finite values.
Results may differ from a plain program's by a relative error of at most 0.02.
The roundings to bfloat16 on the way count: a program that leaves them out, or rounds other values in their place, can miss the bound.
Values may be sent and summed in bfloat16 or wider, within the bound.
A program may use at most 64 MiB of HBM per device.

v0:
```python
import jax
import jax.numpy as jnp
from jax import lax
from jax.sharding import PartitionSpec as P

BX = 32
BY = 16


OFFSETS = [(position // 9, position // 3 % 3, position % 3) for position in range(27)]


def extended(cells, sides, width):
    for axis, dim in sides:
        count = lax.axis_size(axis)
        ends = count - 1
        head = lax.slice_in_dim(cells, 0, width, axis=dim)
        tail = lax.slice_in_dim(cells, cells.shape[dim] - width, cells.shape[dim], axis=dim)
        cells = jnp.concatenate(
            [
                lax.ppermute(tail, axis, [(i, (i + 1) % count) for i in range(ends)]),
                cells,
                lax.ppermute(head, axis, [((i + 1) % count, i) for i in range(ends)]),
            ],
            axis=dim,
        )
    return cells


def leaky(values):
    return jnp.where(values > 0, values, 0.3 * values)


def slope(values):
    return jnp.where(values > 0, 1.0, 0.3)


def pool(values):
    channels, planes, height, breadth = values.shape
    cubes = values.reshape(channels, planes // 2, 2, height // 2, 2, breadth // 2, 2)
    return jnp.sum(cubes, axis=(2, 4, 6)) * 0.125


def upsample(values):
    channels, planes, height, breadth = values.shape
    spread = jnp.broadcast_to(
        values[:, :, None, :, None, :, None], (channels, planes, 2, height, 2, breadth, 2)
    )
    return spread.reshape(channels, planes * 2, height * 2, breadth * 2)


def pad_planes(values):
    return jnp.pad(values, ((0, 0), (1, 1), (0, 0), (0, 0)))


def flip_weight(weight):
    outputs = weight.shape[1]
    channels = weight.shape[2]
    flipped = weight.reshape(3, 3, 3, outputs, channels)[::-1, ::-1, ::-1]
    return flipped.reshape(27, outputs, channels).transpose(0, 2, 1)


def block_size(channels, planes, height, breadth):
    thickness = 1
    while planes % (thickness * 2) == 0 and 108 * channels * thickness * height * breadth <= 2**21:
        thickness = thickness * 2
    return thickness


def columns(padded, start, thickness, height, breadth):
    slab = lax.dynamic_slice_in_dim(padded, start, thickness + 2, 1)
    stacked = jnp.stack(
        [
            slab[
                :,
                offset[0] : offset[0] + thickness,
                offset[1] : offset[1] + height,
                offset[2] : offset[2] + breadth,
            ]
            for offset in OFFSETS
        ],
        0,
    )
    return stacked.reshape(-1, thickness * height * breadth)


def grid_shape(padded):
    return (padded.shape[0], padded.shape[1] - 2, padded.shape[2] - 2, padded.shape[3] - 2)


def convolve(padded, weight):
    channels, planes, height, breadth = grid_shape(padded)
    outputs = weight.shape[1]
    thickness = block_size(channels, planes, height, breadth)
    flat_weight = weight.transpose(1, 0, 2).reshape(outputs, -1)

    def convolve_one_block(block_id):
        patches = columns(padded, block_id * thickness, thickness, height, breadth)
        return jnp.dot(flat_weight, patches, preferred_element_type=jnp.float32).reshape(
            outputs, thickness, height, breadth
        )

    blocks = lax.map(convolve_one_block, jnp.arange(planes // thickness, dtype=jnp.int32))
    return blocks.transpose(1, 0, 2, 3, 4).reshape(outputs, planes, height, breadth)


def forward_and_grad(padded, weight, cotangent):
    channels, planes, height, breadth = grid_shape(padded)
    outputs = weight.shape[1]
    thickness = block_size(channels, planes, height, breadth)
    count = planes // thickness
    flat_weight = weight.transpose(1, 0, 2).reshape(outputs, -1)
    upstream = cotangent.reshape(outputs, count, thickness * height * breadth).transpose(1, 0, 2)

    def forward_one_block(total, pair):
        block_id, incoming = pair
        patches = columns(padded, block_id * thickness, thickness, height, breadth)
        hidden = jnp.dot(flat_weight, patches, preferred_element_type=jnp.float32)
        activated = leaky(hidden).astype(jnp.bfloat16)
        delta = (incoming.astype(jnp.float32) * slope(hidden)).astype(jnp.bfloat16)
        total = total + lax.dot_general(
            delta, patches, (((1,), (1,)), ((), ())), preferred_element_type=jnp.float32
        )
        return (total, (activated, delta))

    start_total = jnp.zeros((outputs, 27 * channels), jnp.float32)
    total, (activated, delta) = lax.scan(
        forward_one_block, start_total, (jnp.arange(count, dtype=jnp.int32), upstream)
    )
    activated = activated.transpose(1, 0, 2).reshape(outputs, planes, height, breadth)
    delta = delta.transpose(1, 0, 2).reshape(outputs, planes, height, breadth)
    return (activated, delta, total.reshape(outputs, 27, channels).transpose(1, 0, 2))


def weight_grad(padded, delta):
    channels, planes, height, breadth = grid_shape(padded)
    outputs = delta.shape[0]
    thickness = block_size(channels, planes, height, breadth)
    count = planes // thickness
    upstream = delta.reshape(outputs, count, thickness * height * breadth).transpose(1, 0, 2)

    def weight_one_block(total, pair):
        block_id, incoming = pair
        patches = columns(padded, block_id * thickness, thickness, height, breadth)
        total = total + lax.dot_general(
            incoming, patches, (((1,), (1,)), ((), ())), preferred_element_type=jnp.float32
        )
        return (total, None)

    start_total = jnp.zeros((outputs, 27 * channels), jnp.float32)
    total, _ = lax.scan(
        weight_one_block, start_total, (jnp.arange(count, dtype=jnp.int32), upstream)
    )
    return total.reshape(outputs, 27, channels).transpose(1, 0, 2)


def per_device(inputs, weight_one, weight_two, cotangent):
    field_in = inputs.reshape(inputs.shape[0], inputs.shape[1], BY, BX)
    upstream = cotangent.reshape(cotangent.shape[0], cotangent.shape[1], BY // 2, BX // 2)
    padded_in = extended(field_in, (("sx", 3), ("sy", 2), ("af", 1)), 1)
    hidden_one = convolve(padded_in, weight_one)
    pooled = pool(leaky(hidden_one)).astype(jnp.bfloat16)
    gathered = lax.all_gather(pooled, "af", axis=1, tiled=True)
    padded_two = pad_planes(extended(gathered, (("sx", 3), ("sy", 2)), 1))
    incoming = lax.all_to_all(upstream, "af", split_axis=0, concat_axis=1, tiled=True)
    activated, delta_two, grad_part = forward_and_grad(padded_two, weight_two, incoming)
    output = lax.all_to_all(activated, "af", split_axis=1, concat_axis=0, tiled=True)
    padded_delta = pad_planes(extended(delta_two, (("sx", 3), ("sy", 2)), 1))
    partial_sum = convolve(padded_delta, flip_weight(weight_two))
    pooled_grad = lax.psum_scatter(partial_sum, "af", scatter_dimension=1, tiled=True).astype(
        jnp.bfloat16
    )
    output = output.reshape(output.shape[0], output.shape[1], 1, 1, -1)
    cell_count = (
        BX * BY * inputs.shape[1] * lax.axis_size("sx") * lax.axis_size("sy") * lax.axis_size("af")
    )
    grad_two = lax.psum(grad_part, ("sx", "sy")) * (cell_count / 8.0) ** (-0.5)
    spread = upsample(pooled_grad.astype(jnp.float32) * 0.125)
    delta_one = (spread * slope(hidden_one)).astype(jnp.bfloat16)
    grad_one = lax.psum(weight_grad(padded_in, delta_one), ("sx", "sy", "af")) * (
        cell_count * 1.0
    ) ** (-0.5)
    return (output, grad_one, grad_two)


def solution(mesh):
    placed = (
        P(None, "af", "sy", "sx", None),
        P(),
        P(None, "af", None),
        P(None, "af", "sy", "sx", None),
    )
    return jax.shard_map(
        per_device,
        mesh=mesh,
        in_specs=placed,
        out_specs=(P(None, "af", "sy", "sx", None), P(), P(None, "af", None)),
        check_vma=False,
    )
```

profile of v0, /device:TPU:1, one launch (start us, length us, event | category | flops | bytes accessed | tf_op | source)
XLA Modules:
  0.0 790.6 jit_solution(727019384708952799)
XLA Ops:
  8.5 8.8 %collective-permute-start.1 = (bf16[32,2,16,1]{3,2,1,0:T(8,128)(2,1)S(1)}, bf16[32,2,16,1]{3,2,1,0:T(8,128)(2,1)S(1)}, u32[]{:S(2)}, u32[]{:S(2)}) collective-permute-start(bf16[32,2,16,1]{3,2,1,0:T(8,128)(2,1)S(1)} %get-tuple-element.212), channel_id=1, source_target_pairs={{128,0},{256,128},{384,256},{129,1},{257,129},{385,257},{130,2},{2... | collective-permute-start | bytes 6152 | tf_op jit(solution)/shard_map/ppermute | solution.py:23
  24.1 4.0 collective-permute-start.2
  30.0 5.8 all-to-all-start
  43.4 4.8 collective-permute-start.4
  82.1 9.7 %reshape.183 = bf16[864,1024]{1,0:T(8,128)(2,1)S(1)} reshape(bf16[27,32,2,16,32]{4,3,2,1,0:T(8,128)(2,1)} %bitcast_dynamic-update-slice_fusion.1) | data formatting | bytes 3538944 | tf_op jit(solution)/shard_map/while/body/eval_jaxpr/reshape | solution.py:84
  93.1 39.6 %all-gather = bf16[64,128,16]{0,2,1:T(8,128)(2,1)S(1)} all-gather(bf16[64,8,16]{0,2,1:T(8,128)(2,1)S(1)} %multiply_convert_fusion.1), channel_id=2, replica_groups=mesh['sx'=4,'sy'=8,'af'=16] {'af'}, dimensions={1}, use_global_device_ids=true | all-gather | bytes 278528 | tf_op jit(solution)/shard_map/all_gather | solution.py:163
  133.4 7.8 collective-permute-start.7
  141.2 6.2 collective-permute-start.6
  173.9 4.6 collective-permute-start.8
  182.9 139.4 %while.3 = (s32[]{:T(128)}, f32[8,1728]{1,0:T(8,128)S(1)}, bf16[4,8,512]{2,1,0:T(8,128)(2,1)}, bf16[4,8,512]{2,1,0:T(8,128)(2,1)}, bf16[4,8,512]{2,1,0:T(8,128)(...) while((s32[]{:T(128)}, f32[8,1728]{1,0:T(8,128)S(1)}, ...), condition=%wide.region_2.3_spmd.clone, body=%wide.region_1.2_spmd.clone.sunk | while | flops 28392460 | bytes 16197101 | solution.py:127
  202.7 8.0 %copy.51 = bf16[27,64,4,8,16]{1,0,4,3,2:T(8,128)(2,1)} copy(bf16[27,64,4,8,16]{1,4,3,2,0:T(8,128)(2,1)} %fusion.159) | data formatting | bytes 3538944 | tf_op jit(solution)/shard_map/while/body/eval_jaxpr/stack | solution.py:72
  210.7 5.5 reshape.204
  237.6 8.0 %copy.51 = bf16[27,64,4,8,16]{1,0,4,3,2:T(8,128)(2,1)} copy(bf16[27,64,4,8,16]{1,4,3,2,0:T(8,128)(2,1)} %fusion.159) | data formatting | bytes 3538944 | tf_op jit(solution)/shard_map/while/body/eval_jaxpr/stack | solution.py:72
  245.6 5.5 reshape.204
  272.4 8.0 %copy.51 = bf16[27,64,4,8,16]{1,0,4,3,2:T(8,128)(2,1)} copy(bf16[27,64,4,8,16]{1,4,3,2,0:T(8,128)(2,1)} %fusion.159) | data formatting | bytes 3538944 | tf_op jit(solution)/shard_map/while/body/eval_jaxpr/stack | solution.py:72
  280.4 5.5 reshape.204
  307.3 8.0 %copy.51 = bf16[27,64,4,8,16]{1,0,4,3,2:T(8,128)(2,1)} copy(bf16[27,64,4,8,16]{1,4,3,2,0:T(8,128)(2,1)} %fusion.159) | data formatting | bytes 3538944 | tf_op jit(solution)/shard_map/while/body/eval_jaxpr/stack | solution.py:72
  315.2 5.5 reshape.204
  325.6 3.6 collective-permute-start.10
  334.4 4.6 collective-permute-start.12
  368.2 12.8 %reshape.189 = bf16[216,2048]{1,0:T(8,128)(2,1)S(1)} reshape(bf16[27,8,16,8,16]{4,3,2,1,0:T(8,128)(2,1)} %fusion.46) | data formatting | bytes 1769472 | tf_op jit(solution)/shard_map/while/body/eval_jaxpr/reshape | solution.py:84
  388.3 8.6 %all-to-all-start.1 = ((bf16[16,2,512]{2,1,0:T(2,128)(2,1)}), bf16[16,2,512]{2,1,0:T(2,128)(2,1)S(1)}, u32[]{:S(2)}, u32[]{:S(2)}) async-start(bf16[16,2,512]{2,1,0:T(2,128)(2,1)} %reshape.201), calls=%async_computation.1 | async-start | bytes 65536 | tf_op jit(solution)/shard_map/all_to_all | solution.py:167
  397.0 108.6 %psum.15 = f32[27,8,64]{2,0,1:T(8,128)S(1)} all-reduce(f32[27,8,64]{2,0,1:T(8,128)S(1)} %bitcast.478), channel_id=1, replica_groups=mesh['sx'=4,'sy'=8,'af'=16] {'sx','sy'}, use_global_device_ids=true, to_apply=%region_5.6 | all-reduce | flops 13824 | bytes 110592 | tf_op jit(solution)/shard_map/psum | solution.py:177
  510.1 271.7 %all-reduce.4.cloned.1.call-done = f32[27,64,32]{1,2,0:T(8,128)} async-done(((f32[27,64,32]{1,2,0:T(8,128)}), f32[27,64,32]{1,2,0:T(8,128)}) %all-reduce.4.cloned.1.call-update) | async-done | bytes 221200 | tf_op jit(solution)/shard_map/psum | solution.py:180
  (340 shorter events, 218.0 us)
Async XLA Ops:
  7.2 84.6 %copy-start = (bf16[27,64,32]{1,2,0:T(8,128)(2,1)S(1)}, bf16[27,64,32]{1,2,0:T(8,128)(2,1)}, u32[]{:S(2)}) copy-start(bf16[27,64,32]{1,2,0:T(8,128)(2,1)} %param.7) | copy-start | bytes 331780
  8.5 10.7 %collective-permute-start.1 = (bf16[32,2,16,1]{3,2,1,0:T(8,128)(2,1)S(1)}, bf16[32,2,16,1]{3,2,1,0:T(8,128)(2,1)S(1)}, u32[]{:S(2)}, u32[]{:S(2)}) collective-permute-start(bf16[32,2,16,1]{3,2,1,0:T(8,128)(2,1)S(1)} %get-tuple-element.212), channel_id=1, source_target_pairs={{128,0},{256,128},{384,256},{129,1},{257,129},{385,257},{130,2},{2... | collective-permute-start | bytes 6152 | tf_op jit(solution)/shard_map/ppermute | solution.py:23
  17.3 5.2 collective-permute-start
  22.8 18.0 %collective-permute-start.3 = (bf16[32,2,1,34]{3,2,1,0:T(2,128)(2,1)S(1)}, bf16[32,2,1,34]{3,2,1,0:T(2,128)(2,1)S(1)}, u32[]{:S(2)}, u32[]{:S(2)}) collective-permute-start(bf16[32,2,1,34]{3,2,1,0:T(2,128)(2,1)S(1)} %get-tuple-element.178), channel_id=1, source_target_pairs={{16,0},{32,16},{48,32},{64,48},{80,64},{96,80},{112,96},{17,1},{33... | collective-permute-start | bytes 13064 | tf_op jit(solution)/shard_map/ppermute | solution.py:23
  24.1 16.7 %collective-permute-start.2 = (bf16[32,2,1,34]{3,2,1,0:T(2,128)(2,1)S(1)}, bf16[32,2,1,34]{3,2,1,0:T(2,128)(2,1)S(1)}, u32[]{:S(2)}, u32[]{:S(2)}) collective-permute-start(bf16[32,2,1,34]{3,2,1,0:T(2,128)(2,1)S(1)} %get-tuple-element.177), channel_id=1, source_target_pairs={{0,16},{16,32},{32,48},{48,64},{64,80},{80,96},{96,112},{1,17},{17... | collective-permute-start | bytes 13064 | tf_op jit(solution)/shard_map/ppermute | solution.py:21
  30.0 150.1 %all-to-all-start = ((bf16[16,2,512]{2,1,0:T(2,128)(2,1)}), bf16[16,2,512]{2,1,0:T(2,128)(2,1)}, u32[]{:S(2)}, u32[]{:S(2)}) async-start(bf16[16,2,512]{2,1,0:T(2,128)(2,1)} %reshape.199), calls=%async_computation | async-start | bytes 65536 | tf_op jit(solution)/shard_map/all_to_all | solution.py:165
  35.8 470.8 %reduce-scatter.2.cloned.1.call-start = ((), (), s32[]{:S(2)}) async-start(), calls=%async_computation.3 | async-start | bytes 1114112 | tf_op jit(solution)/shard_map/reduce_scatter | solution.py:170
  42.1 12.1 %collective-permute-start.5 = (bf16[32,1,18,34]{3,2,1,0:T(8,128)(2,1)}, bf16[32,1,18,34]{3,2,1,0:T(8,128)(2,1)}, u32[]{:S(2)}, u32[]{:S(2)}) collective-permute-start(bf16[32,1,18,34]{3,2,1,0:T(8,128)(2,1)} %get-tuple-element.207), channel_id=1, source_target_pairs={{1,0},{2,1},{3,2},{4,3},{5,4},{6,5},{7,6},{8,7},{9,8},{10,9},{11,1... | collective-permute-start | bytes 117512 | tf_op jit(solution)/shard_map/ppermute | solution.py:23
  43.4 10.8 %collective-permute-start.4 = (bf16[32,1,18,34]{3,2,1,0:T(8,128)(2,1)}, bf16[32,1,18,34]{3,2,1,0:T(8,128)(2,1)}, u32[]{:S(2)}, u32[]{:S(2)}) collective-permute-start(bf16[32,1,18,34]{3,2,1,0:T(8,128)(2,1)} %get-tuple-element.208), channel_id=1, source_target_pairs={{0,1},{1,2},{2,3},{3,4},{4,5},{5,6},{6,7},{7,8},{8,9},{9,10},{10,1... | collective-permute-start | bytes 117512 | tf_op jit(solution)/shard_map/ppermute | solution.py:21
  92.3 64.7 %copy-start.8 = (bf16[32,2,16,32]{3,2,1,0:T(8,128)(2,1)S(1)}, bf16[32,2,16,32]{3,2,1,0:T(8,128)(2,1)}, u32[]{:S(2)}) copy-start(bf16[32,2,16,32]{3,2,1,0:T(8,128)(2,1)} %get-tuple-element.165) | copy-start | bytes 196612
  92.3 65.0 %copy-start.9 = (bf16[32,2,16,32]{3,2,1,0:T(8,128)(2,1)S(1)}, bf16[32,2,16,32]{3,2,1,0:T(8,128)(2,1)}, u32[]{:S(2)}) copy-start(bf16[32,2,16,32]{3,2,1,0:T(8,128)(2,1)} %get-tuple-element.163) | copy-start | bytes 196612
  92.5 78.0 %copy-start.11 = (bf16[1,32,1024]{2,1,0:T(8,128)(2,1)S(1)}, bf16[1,32,1024]{2,1,0:T(8,128)(2,1)}, u32[]{:S(2)}) copy-start(bf16[1,32,1024]{2,1,0:T(8,128)(2,1)} %stack.491) | copy-start | bytes 196612
  92.5 78.6 %copy-start.10 = (bf16[1,32,1024]{2,1,0:T(8,128)(2,1)S(1)}, bf16[1,32,1024]{2,1,0:T(8,128)(2,1)}, u32[]{:S(2)}) copy-start(bf16[1,32,1024]{2,1,0:T(8,128)(2,1)} %stack.492) | copy-start | bytes 196612
  133.4 38.3 %collective-permute-start.7 = (bf16[64,16,8,1]{0,3,2,1:T(2,128)(2,1)}, bf16[64,16,8,1]{0,3,2,1:T(2,128)(2,1)}, u32[]{:S(2)}, u32[]{:S(2)}) collective-permute-start(bf16[64,16,8,1]{0,3,2,1:T(2,128)(2,1)} %get-tuple-element.200), channel_id=1, source_target_pairs={{128,0},{256,128},{384,256},{129,1},{257,129},{385,257},{130,2},{2... | collective-permute-start | bytes 49160 | tf_op jit(solution)/shard_map/ppermute | solution.py:23
  141.2 30.5 %collective-permute-start.6 = (bf16[64,16,8,1]{0,3,2,1:T(2,128)(2,1)}, bf16[64,16,8,1]{0,3,2,1:T(2,128)(2,1)}, u32[]{:S(2)}, u32[]{:S(2)}) collective-permute-start(bf16[64,16,8,1]{0,3,2,1:T(2,128)(2,1)} %get-tuple-element.199), channel_id=1, source_target_pairs={{0,128},{128,256},{256,384},{1,129},{129,257},{257,385},{2,130},{1... | collective-permute-start | bytes 49160 | tf_op jit(solution)/shard_map/ppermute | solution.py:21
  172.6 8.8 %collective-permute-start.9 = (bf16[64,16,1,18]{0,3,2,1:T(8,128)(2,1)S(1)}, bf16[64,16,1,18]{0,3,2,1:T(8,128)(2,1)S(1)}, u32[]{:S(2)}, u32[]{:S(2)}) collective-permute-start(bf16[64,16,1,18]{0,3,2,1:T(8,128)(2,1)S(1)} %get-tuple-element.180), channel_id=1, source_target_pairs={{16,0},{32,16},{48,32},{64,48},{80,64},{96,80},{112,96},{17,1},{33... | collective-permute-start | bytes 110600 | tf_op jit(solution)/shard_map/ppermute | solution.py:23
  173.9 7.5 collective-permute-start.8
  323.5 8.5 %collective-permute-start.11 = (bf16[8,16,8,1]{3,2,1,0:T(8,128)(2,1)S(1)}, bf16[8,16,8,1]{3,2,1,0:T(8,128)(2,1)S(1)}, u32[]{:S(2)}, u32[]{:S(2)}) collective-permute-start(bf16[8,16,8,1]{3,2,1,0:T(8,128)(2,1)S(1)} %get-tuple-element.210), channel_id=1, source_target_pairs={{128,0},{256,128},{384,256},{129,1},{257,129},{385,257},{130,2},{2... | collective-permute-start | bytes 6152 | tf_op jit(solution)/shard_map/ppermute | solution.py:23
  325.6 6.9 collective-permute-start.10
  333.1 10.7 %collective-permute-start.13 = (bf16[8,16,1,18]{3,2,1,0:T(2,128)(2,1)S(1)}, bf16[8,16,1,18]{3,2,1,0:T(2,128)(2,1)S(1)}, u32[]{:S(2)}, u32[]{:S(2)}) collective-permute-start(bf16[8,16,1,18]{3,2,1,0:T(2,128)(2,1)S(1)} %get-tuple-element.174), channel_id=1, source_target_pairs={{16,0},{32,16},{48,32},{64,48},{80,64},{96,80},{112,96},{17,1},{33... | collective-permute-start | bytes 13832 | tf_op jit(solution)/shard_map/ppermute | solution.py:23
  334.4 9.4 %collective-permute-start.12 = (bf16[8,16,1,18]{3,2,1,0:T(2,128)(2,1)S(1)}, bf16[8,16,1,18]{3,2,1,0:T(2,128)(2,1)S(1)}, u32[]{:S(2)}, u32[]{:S(2)}) collective-permute-start(bf16[8,16,1,18]{3,2,1,0:T(2,128)(2,1)S(1)} %get-tuple-element.173), channel_id=1, source_target_pairs={{0,16},{16,32},{32,48},{48,64},{64,80},{80,96},{96,112},{1,17},{17... | collective-permute-start | bytes 13832 | tf_op jit(solution)/shard_map/ppermute | solution.py:21
  387.1 120.8 %copy-start.1 = (bf16[27,32,1024]{2,1,0:T(8,128)(2,1)S(1)}, bf16[27,32,1024]{2,1,0:T(8,128)(2,1)}, u32[]{:S(2)}) copy-start(bf16[27,32,1024]{2,1,0:T(8,128)(2,1)} %constant_dynamic-update-slice_fusion.2) | copy-start | bytes 5308420
  388.3 118.0 %all-to-all-start.1 = ((bf16[16,2,512]{2,1,0:T(2,128)(2,1)}), bf16[16,2,512]{2,1,0:T(2,128)(2,1)S(1)}, u32[]{:S(2)}, u32[]{:S(2)}) async-start(bf16[16,2,512]{2,1,0:T(2,128)(2,1)} %reshape.201), calls=%async_computation.1 | async-start | bytes 65536 | tf_op jit(solution)/shard_map/all_to_all | solution.py:167
  396.9 384.9 %all-reduce.4.cloned.1.call-start = ((), (), s32[]{:S(2)}) async-start(), calls=%async_computation.4 | async-start | bytes 884736 | tf_op jit(solution)/shard_map/psum | solution.py:180
  (9 other events, 164.1 us)
Sparse Core Ops, SparseCore 0:
  382.8 95.6 reduce-scatter.1
  509.4 272.3 all-reduce.3
where the time goes:
time: 796 us; the launch traced here: 791 us
  waiting for transfers between devices  276 us (35%)
  local copies, waits for them, and re-layouts  257 us (32%)
  blocking collectives  148 us (19%)
  starting transfers between devices  68.1 us (9%)
  other arithmetic  15.4 us (2%)
  between operations  14.9 us (2%)
  matrix products  8.34 us (1%)
    psum x1, waiting for transfers between devices, per_device(): lax.psum(weight_grad(padded_in, delta_one), ('sx', 'sy', 'af'))  272 us
    psum x1, blocking collectives, per_device(): grad_two = lax.psum(grad_part, ('sx', 'sy')) * (cell_count / 8.0) ** (-0.5)  109 us
    while x104, local copies, waits for them, and re-layouts  71.6 us
    unnamed x111, local copies, waits for them, and re-layouts  65.7 us
    another operation x40, local copies, waits for them, and re-layouts, columns(): jnp.stack([slab[:, offset[0]:offset[0] + thickness, offset[1]:offset[1] +...  60.7 us
    reshape x6, local copies, waits for them, and re-layouts, columns(): return stacked.reshape(-1, thickness * height * breadth)  44.3 us
    all_gather x1, blocking collectives, per_device(): gathered = lax.all_gather(pooled, 'af', axis=1, tiled=True)  39.6 us
    ppermute x7, starting transfers between devices, extended(): lax.ppermute(tail, axis, [(i, (i + 1) % count) for i in range(ends)])  29.9 us
  transfers between devices with their start and end apart: 18, of which 3 were waited for; matrix products, arithmetic and copies ran while one was open for 12% of the time, Pallas kernels for 0%

commit v1 on v0

v1 whole, which is shorter than its diff:
```python
import functools

import jax
import jax.numpy as jnp
from jax import lax
from jax.experimental import pallas as pl
from jax.experimental.pallas import tpu as pltpu
from jax.sharding import PartitionSpec as P

MESH = pl.DeviceIdType.MESH
BF16 = jnp.bfloat16
F32 = jnp.float32
N_SX, N_SY, N_AF = 4, 8, 16
SLOTS = [(dx, dy) for dy in (-1, 0, 1) for dx in (-1, 0, 1) if (dx, dy) != (0, 0)]


def iota(shape, axis):
    return lax.broadcasted_iota(jnp.int32, shape, axis)


def leaky(values):
    return jnp.where(values > 0, values, 0.3 * values)


def slope(values):
    return jnp.where(values > 0, 1.0, 0.3)


def one_hot(rows, source):
    return (iota((rows, source.shape[1]), 0) == source).astype(F32).astype(BF16)


def dot(a, b):
    return jnp.dot(a, b, preferred_element_type=F32)


def dot_nt(a, b):
    return lax.dot_general(a, b, (((1,), (1,)), ((), ())), preferred_element_type=F32)


def rolled(values, shift):
    shift = shift % values.shape[1]
    return values if shift == 0 else pltpu.roll(values, shift, 1)


def border_selection_one():
    lane = iota((1, 128), 1)
    source = jnp.full((1, 128), -1, jnp.int32)
    source = jnp.where(lane == 0, 511, source)
    source = jnp.where((lane >= 1) & (lane <= 16), 32 * (lane - 1) + 31, source)
    source = jnp.where(lane == 17, 31, source)
    source = jnp.where((lane >= 32) & (lane < 64), 480 + lane - 32, source)
    source = jnp.where(lane == 64, 480, source)
    source = jnp.where((lane >= 65) & (lane <= 80), 32 * (lane - 65), source)
    source = jnp.where(lane == 81, 0, source)
    source = jnp.where(lane >= 96, lane - 96, source)
    return one_hot(512, source)


def column_placement_one():
    lane = iota((1, 1536), 1)
    offset = lane // 512
    y = lane % 512 // 32
    x = lane % 32
    source = jnp.where(x == 0, y + offset, jnp.where(x == 31, 64 + y + offset, -1))
    return one_hot(128, source)


def border_selection_two():
    lane = iota((1, 256), 1)
    plane = lane % 128 // 32
    r = lane % 32
    rows = jnp.where(r < 16, 112 + r, r - 16)
    columns = jnp.full((1, 256), -1000, jnp.int32)
    columns = jnp.where(r == 0, 127, columns)
    columns = jnp.where((r >= 1) & (r <= 8), 16 * (r - 1) + 15, columns)
    columns = jnp.where(r == 9, 15, columns)
    columns = jnp.where(r == 16, 112, columns)
    columns = jnp.where((r >= 17) & (r <= 24), 16 * (r - 17), columns)
    columns = jnp.where(r == 25, 0, columns)
    source = 128 * plane + jnp.where(lane < 128, rows, columns)
    return one_hot(384, jnp.where(plane < 3, source, -1))


def column_placement_two():
    lane = iota((1, 1152), 1)
    plane = lane // 384
    offset = lane // 128 % 3
    y = lane % 128 // 16
    x = lane % 16
    source = jnp.where(x == 0, y + offset, jnp.where(x == 15, 16 + y + offset, -1000))
    return one_hot(128, 32 * plane + source)


def pool_selection():
    lane = iota((1, 128), 1)
    return one_hot(512, 64 * (lane // 16) + 2 * (lane % 16))


def spread_selection():
    lane = iota((1, 512), 1)
    return one_hot(128, 16 * (lane // 64) + lane % 32 // 2)


def kernel(
    x_ref, w1_ref, w2_ref, cot_ref,
    out_ref, grad_one_ref, grad_two_ref,
    x_all, w1_cat, w2_all, pack_one, recv_one, patches_one, hidden_one,
    p_all, pack_p, recv_p, patches_two,
    d_all, pack_d, recv_d, w2_turned, patches_d,
    g2_send, g2_recv, g2_tiles, g2_sy, g2_sx, g2_done,
    g1_full, g1_send, g1_sx, g1_tiles, g1_sy, g1_af, g1_part, g1_done,
    z_sems, plane_sems, w2_sems, g2_sems, g2_sy_sems, g2_sx_sems, g2_done_sems,
    g1_sx_sems, g1_sy_sems, g1_af_sems, g1_part_sems, g1_done_sems,
):
    sx, sy, af = lax.axis_index("sx"), lax.axis_index("sy"), lax.axis_index("af")

    barrier = pltpu.get_barrier_semaphore()
    for axis, me, count in (("sx", sx, N_SX), ("sy", sy, N_SY), ("af", af, N_AF)):

        def greet(j, carry, axis=axis, me=me, count=count):
            pl.semaphore_signal(
                barrier, inc=1, device_id={axis: lax.rem(me + j, count)}, device_id_type=MESH
            )
            return carry

        lax.fori_loop(1, count, greet, 0)
    for dx in (1, N_SX - 1):
        for dy in (1, N_SY - 1):
            pl.semaphore_signal(
                barrier,
                inc=1,
                device_id={"sx": lax.rem(sx + dx, N_SX), "sy": lax.rem(sy + dy, N_SY)},
                device_id_type=MESH,
            )
    pl.semaphore_wait(barrier, N_SX + N_SY + N_AF + 1)

    pending = []

    class Ring:
        def __init__(self, axis, me, count, source, target, sems):
            self.count = count

            def copy(j):
                peer = lax.rem(me + j, count)
                return pltpu.make_async_remote_copy(
                    src_ref=source(peer),
                    dst_ref=target.at[me],
                    send_sem=sems.at[0, j],
                    recv_sem=sems.at[1, j],
                    device_id={axis: peer},
                    device_id_type=MESH,
                )

            self.copy = copy
            self.each(lambda copy: copy.start())
            pending.append(self.wait_send)

        def each(self, act):
            def body(j, carry):
                act(self.copy(j))
                return carry

            lax.fori_loop(1, self.count, body, 0)

        def wait_recv(self):
            self.each(lambda copy: copy.wait_recv())

        def wait_send(self):
            self.each(lambda copy: copy.wait_send())

    def exchange_planes(low, high, target, index):
        last = target.shape[0] - 1
        copies = [
            pltpu.make_async_remote_copy(
                src_ref=source,
                dst_ref=target.at[slot],
                send_sem=z_sems.at[0, index, way],
                recv_sem=z_sems.at[1, index, way],
                device_id={"af": lax.rem(af + step, N_AF)},
                device_id_type=MESH,
            )
            for way, (source, slot, step) in enumerate(((low, last, N_AF - 1), (high, 0, 1)))
        ]
        for copy in copies:
            copy.start()
            pending.append(copy.wait_send)
        return copies

    def exchange_borders(source, target, index):
        copies = []
        for slot, (dx, dy) in enumerate(SLOTS):
            copy = pltpu.make_async_remote_copy(
                src_ref=source(dx, dy),
                dst_ref=target.at[slot],
                send_sem=plane_sems.at[0, index, slot],
                recv_sem=plane_sems.at[1, index, slot],
                device_id={
                    "sx": lax.rem(sx + N_SX - dx, N_SX),
                    "sy": lax.rem(sy + N_SY - dy, N_SY),
                },
                device_id_type=MESH,
            )
            copy.start()
            pending.append(copy.wait_send)
            copies.append(copy)
        return copies

    def inside(dx, dy):
        good = True
        if dx:
            good = (sx > 0) if dx < 0 else (sx < N_SX - 1)
        if dy:
            row = (sy > 0) if dy < 0 else (sy < N_SY - 1)
            good = row if good is True else good & row
        return good

    def gather_columns(received, height, right):
        first = received[0].astype(F32)
        lane = iota(first.shape, 1)
        r = lane if right == 64 else lane % 32
        columns = jnp.zeros(first.shape, F32)
        for dx, start in ((-1, 0), (1, right)):
            for dy, cells in (
                (0, (r >= start + 1) & (r <= start + height)),
                (-1, r == start),
                (1, r == start + height + 1),
            ):
                values = received[SLOTS.index((dx, dy))].astype(F32)
                columns = jnp.where(cells & inside(dx, dy), values, columns)
        return columns.astype(BF16)

    def masked_rows(received, dy):
        values = received[SLOTS.index((0, dy))].astype(F32)
        return jnp.where(inside(0, dy), values, 0.0)

    x_copies = exchange_planes(x_ref.at[0], x_ref.at[1], x_all, 0)
    w2_ring = Ring("af", af, N_AF, lambda peer: w2_ref, w2_all, w2_sems)
    w2_all[af] = w2_ref[...]
    x_all[1] = x_ref[0]
    x_all[2] = x_ref[1]
    for k in range(27):
        w1_cat[:, 32 * k : 32 * k + 32] = w1_ref[k]
    selection = border_selection_one()
    for copy in x_copies:
        copy.wait_recv()

    field = x_all[...].reshape(128, 512).astype(F32)
    row = iota((128, 512), 0)
    outer = ((row < 32) & (af == 0)) | ((row >= 96) & (af == N_AF - 1))
    field = jnp.where(outer, 0.0, field)
    pack_one[...] = dot(field.astype(BF16), selection).astype(BF16)
    copies = exchange_borders(lambda dx, dy: pack_one, recv_one, 0)
    placement = column_placement_one()
    for copy in copies:
        copy.wait_recv()
    columns = dot(gather_columns(recv_one, 16, 64), placement)
    above, below = masked_rows(recv_one, -1), masked_rows(recv_one, 1)
    lane = iota((128, 128), 1)
    x = iota((128, 512), 1) % 32
    for b in range(3):
        for c in range(3):
            dy, dx = b - 1, c - 1
            moved = rolled(field, -(32 * dy + dx))
            if dy == -1:
                first = jnp.where(lane < 32, rolled(above, -(32 + dx)), moved[:, :128])
                moved = jnp.concatenate([first, moved[:, 128:]], axis=1)
            if dy == 1:
                final = jnp.where(lane >= 96, rolled(below, -dx), moved[:, 384:])
                moved = jnp.concatenate([moved[:, :384], final], axis=1)
            if dx:
                placed = columns[:, 512 * b : 512 * b + 512]
                moved = jnp.where(x == (0 if dx < 0 else 31), placed, moved)
            moved = moved.astype(BF16)
            start = 32 * (3 * b + c)
            for z in range(4):
                patches_one[288 * z + start : 288 * z + start + 32] = moved[32 * z : 32 * z + 32]
    total = None
    for z in range(2):
        hidden = dot(w1_cat[...], patches_one[288 * z : 288 * z + 864])
        hidden_one[z] = hidden
        total = leaky(hidden) if total is None else total + leaky(hidden)
    total = total + rolled(total, -1)
    total = total + rolled(total, -32)
    pooled = dot((total * 0.125).astype(BF16), pool_selection()).astype(BF16)

    def second_shifts(field_all, pack, received, index, visit):
        channels = field_all.shape[1]
        planes = []
        for z in range(3):
            values = field_all[z].astype(F32)
            if z != 1:
                values = jnp.where(af > 0 if z == 0 else af < N_AF - 1, values, 0.0)
            planes.append(values)
        joined = jnp.concatenate([values.astype(BF16) for values in planes], axis=1)
        packed = dot(joined, border_selection_two()).astype(BF16)
        pack[0] = packed[:, :128]
        pack[1] = packed[:, 128:]
        copies = exchange_borders(lambda dx, dy: pack.at[0 if dx == 0 else 1], received, index)
        placement = column_placement_two()
        for copy in copies:
            copy.wait_recv()
        columns = dot(gather_columns(received, 8, 16), placement)
        above, below = masked_rows(received, -1), masked_rows(received, 1)
        lane = iota((channels, 128), 1)
        x = lane % 16
        for k in range(27):
            z, dy, dx = k // 9, k // 3 % 3 - 1, k % 3 - 1
            moved = rolled(planes[z], -(16 * dy + dx))
            if dy == -1:
                moved = jnp.where(lane < 16, rolled(above, -(32 * z + dx)), moved)
            if dy == 1:
                moved = jnp.where(lane >= 112, rolled(below, 96 - 32 * z - dx), moved)
            if dx:
                place = 128 * (k // 3)
                moved = jnp.where(
                    x == (0 if dx < 0 else 15), columns[:, place : place + 128], moved
                )
            visit(k, moved)

    p_all[1] = pooled
    copies = exchange_planes(p_all.at[1], p_all.at[1], p_all, 1)
    for copy in copies:
        copy.wait_recv()

    def keep_pooled(k, values):
        half, place = k // 14, k % 14
        patches_two[64 * place : 64 * place + 64, 128 * half : 128 * half + 128] = values.astype(BF16)

    patches_two[832:896, 128:256] = jnp.zeros((64, 128), BF16)
    second_shifts(p_all, pack_p, recv_p, 1, keep_pooled)
    w2_ring.wait_recv()
    filters = w2_all[...].reshape(256, 896)
    product = dot(filters, patches_two[...]).reshape(16, 2, 8, 256)
    hidden_two = (product[:, 0, :, :128] + product[:, 1, :, 128:]).reshape(128, 128)
    out_ref[...] = leaky(hidden_two).astype(BF16)
    delta_two = (cot_ref[...].astype(F32) * slope(hidden_two)).astype(BF16)
    d_all[1] = delta_two
    copies = exchange_planes(d_all.at[1], d_all.at[1], d_all, 2)

    halves = [
        dot_nt(delta_two, patches_two[:, 128 * half : 128 * half + 128]).reshape(16, 1, 8, 896)
        for half in range(2)
    ]
    g2_send[...] = jnp.concatenate(halves, axis=1).reshape(16, 16, 896).astype(BF16)
    turned = filters.astype(F32).T.astype(BF16)
    for place in range(14):
        w2_turned[:, 256 * place : 256 * place + 256] = turned[64 * place : 64 * place + 64]
    for copy in copies:
        copy.wait_recv()
    held = {}

    def keep_delta(k, values):
        held[26 - k] = values.reshape(16, 1, 8, 128)

    second_shifts(d_all, pack_d, recv_d, 2, keep_delta)
    g2_ring = Ring("af", af, N_AF, lambda peer: g2_send.at[peer], g2_recv, g2_sems)
    g2_recv[af] = g2_send[af]
    held[27] = jnp.zeros((16, 1, 8, 128), F32)
    for place in range(14):
        both = jnp.concatenate([held[place], held[place + 14]], axis=1)
        patches_d[256 * place : 256 * place + 256] = both.reshape(256, 128).astype(BF16)
    pooled_grad = dot(w2_turned[...], patches_d[...]).astype(BF16)

    spread = dot(pooled_grad, spread_selection()) * 0.125
    total = None
    for z in range(2):
        delta_one = (spread * slope(hidden_one[z])).astype(BF16)
        part = dot_nt(delta_one, patches_one[288 * z : 288 * z + 864])
        total = part if total is None else total + part
    g1_full[...] = jnp.zeros((64, 896), F32)
    g1_full[:, :864] = total
    g1_send[...] = g1_full[...].astype(BF16).reshape(4, 16, 896)
    g1_sx_ring = Ring("sx", sx, N_SX, lambda peer: g1_send.at[peer], g1_sx, g1_sx_sems)
    g1_sx[sx] = g1_send[sx]

    def to_tiles(values, tiles):
        for t in range(7):
            tiles[t] = values[:, 128 * t : 128 * t + 128]
        tiles[7] = jnp.zeros((16, 128), F32)

    g2_ring.wait_recv()
    to_tiles(jnp.sum(g2_recv[...].astype(F32), axis=0), g2_tiles)
    g2_sy_ring = Ring("sy", sy, N_SY, lambda peer: g2_tiles.at[peer], g2_sy, g2_sy_sems)
    g2_sy[sy] = g2_tiles[sy]

    g1_sx_ring.wait_recv()
    to_tiles(jnp.sum(g1_sx[...].astype(F32), axis=0), g1_tiles)
    g1_sy_ring = Ring("sy", sy, N_SY, lambda peer: g1_tiles.at[peer], g1_sy, g1_sy_sems)
    g1_sy[sy] = g1_tiles[sy]

    g2_sy_ring.wait_recv()
    g2_sx[sx] = jnp.sum(g2_sy[...], axis=0)
    g2_sx_ring = Ring("sx", sx, N_SX, lambda peer: g2_sx.at[sx], g2_sx, g2_sx_sems)

    g1_sy_ring.wait_recv()
    g1_af[af] = jnp.sum(g1_sy[...], axis=0)
    g1_af_ring = Ring("af", af, N_AF, lambda peer: g1_af.at[af], g1_af, g1_af_sems)

    g2_sx_ring.wait_recv()
    g2_done[sy] = jnp.sum(g2_sx[...], axis=0) * (1.0 / 256.0)
    g2_done_ring = Ring("sy", sy, N_SY, lambda peer: g2_done.at[sy], g2_done, g2_done_sems)

    g1_af_ring.wait_recv()
    g1_part[sy] = jnp.sum(g1_af[...], axis=0) * (524288.0**-0.5)
    g1_part_ring = Ring("sy", sy, N_SY, lambda peer: g1_part.at[sy], g1_part, g1_part_sems)

    g2_done_ring.wait_recv()
    for k in range(27):
        half, place = k // 14, k % 14
        tile = g2_done[place // 2, 8 * half : 8 * half + 8]
        grad_two_ref[k] = tile[:, 64 * (place % 2) : 64 * (place % 2) + 64]

    g1_part_ring.wait_recv()
    g1_done_ring = Ring("sx", sx, N_SX, lambda peer: g1_part, g1_done, g1_done_sems)
    g1_done[sx] = g1_part[...]
    g1_done_ring.wait_recv()
    for k in range(27):
        for q in range(4):
            tile = g1_done[q, k // 4]
            grad_one_ref[k, 16 * q : 16 * q + 16] = tile[:, 32 * (k % 4) : 32 * (k % 4) + 32]

    for wait in pending:
        wait()


def per_device(inputs, weight_one, weight_two, cotangent):
    x = inputs.reshape(32, 2, 512).transpose(1, 0, 2)
    cot = cotangent.reshape(128, 128)
    w2 = jnp.pad(weight_two, ((0, 1), (0, 0), (0, 0)))
    w2 = w2.reshape(2, 14, 8, 64).transpose(0, 2, 1, 3).reshape(16, 896)
    vmem = pl.BlockSpec(memory_space=pltpu.VMEM)
    ring_sems = [pltpu.SemaphoreType.DMA((2, n)) for n in (16, 16, 8, 4, 8, 4, 8, 16, 8, 4)]
    output, grad_one, grad_two = pl.pallas_call(
        kernel,
        out_shape=(
            jax.ShapeDtypeStruct((128, 128), BF16),
            jax.ShapeDtypeStruct((27, 64, 32), F32),
            jax.ShapeDtypeStruct((27, 8, 64), F32),
        ),
        in_specs=[vmem] * 4,
        out_specs=(vmem, vmem, vmem),
        scratch_shapes=[
            pltpu.VMEM((4, 32, 512), BF16),
            pltpu.VMEM((64, 864), BF16),
            pltpu.VMEM((16, 16, 896), BF16),
            pltpu.VMEM((128, 128), BF16),
            pltpu.VMEM((8, 128, 128), BF16),
            pltpu.VMEM((1152, 512), BF16),
            pltpu.VMEM((2, 64, 512), F32),
            pltpu.VMEM((3, 64, 128), BF16),
            pltpu.VMEM((2, 64, 128), BF16),
            pltpu.VMEM((8, 64, 128), BF16),
            pltpu.VMEM((896, 256), BF16),
            pltpu.VMEM((3, 128, 128), BF16),
            pltpu.VMEM((2, 128, 128), BF16),
            pltpu.VMEM((8, 128, 128), BF16),
            pltpu.VMEM((64, 3584), BF16),
            pltpu.VMEM((3584, 128), BF16),
            pltpu.VMEM((16, 16, 896), BF16),
            pltpu.VMEM((16, 16, 896), BF16),
            pltpu.VMEM((8, 16, 128), F32),
            pltpu.VMEM((8, 16, 128), F32),
            pltpu.VMEM((4, 16, 128), F32),
            pltpu.VMEM((8, 16, 128), F32),
            pltpu.VMEM((64, 896), F32),
            pltpu.VMEM((4, 16, 896), BF16),
            pltpu.VMEM((4, 16, 896), BF16),
            pltpu.VMEM((8, 16, 128), F32),
            pltpu.VMEM((8, 16, 128), F32),
            pltpu.VMEM((16, 16, 128), F32),
            pltpu.VMEM((8, 16, 128), F32),
            pltpu.VMEM((4, 8, 16, 128), F32),
            pltpu.SemaphoreType.DMA((2, 3, 2)),
            pltpu.SemaphoreType.DMA((2, 3, 8)),
            *ring_sems,
        ],
        compiler_params=pltpu.CompilerParams(
            collective_id=0, has_side_effects=True, vmem_limit_bytes=48 * 2**20
        ),
    )(x, weight_one, w2, cot)
    return output.reshape(128, 1, 1, 1, 128), grad_one, grad_two


def solution(mesh):
    placed = (
        P(None, "af", "sy", "sx", None),
        P(),
        P(None, "af", None),
        P(None, "af", "sy", "sx", None),
    )
    return jax.shard_map(
        per_device,
        mesh=mesh,
        in_specs=placed,
        out_specs=(P(None, "af", "sy", "sx", None), P(), P(None, "af", None)),
        check_vma=False,
    )
```

time: 796 us -> 94.8 us (0.12)
  waiting for transfers between devices: 276 us -> 0 us
  local copies, waits for them, and re-layouts: 257 us -> 4.79 us
  blocking collectives: 148 us -> 0 us
  Pallas kernels: 0 us -> 87.9 us
  starting transfers between devices: 68.1 us -> 0 us
  other arithmetic: 15.4 us -> 0 us
  between operations: 14.9 us -> 0.69 us
  matrix products: 8.34 us -> 0 us
    psum x1 -> x0, waiting for transfers between devices: 272 us -> none  [per_device(): lax.psum(weight_grad(padded_in, delta_one), ('sx', 'sy', 'af'))]
    psum x1 -> x0, blocking collectives: 109 us -> none  [per_device(): grad_two = lax.psum(grad_part, ('sx', 'sy')) * (cell_count / 8.0) ** (-0.5)]
    pallas_call x0 -> x1, Pallas kernels: none -> 87.9 us  [per_device(): pl.pallas_call(kernel, out_shape=(jax.ShapeDtypeStruct((128, 128), BF16),...]
    while x104 -> x0, local copies, waits for them, and re-layouts: 71.6 us -> none
    unnamed x111 -> x11, local copies, waits for them, and re-layouts: 65.7 us -> 3.8 us
    another operation x40 -> x0, local copies, waits for them, and re-layouts: 60.7 us -> none  [columns(): jnp.stack([slab[:, offset[0]:offset[0] + thickness, offset[1]:offset[1] +...]
    ppermute x14 -> x0, starting transfers between devices: 53.7 us -> none  [the longest x7 29.9 us: extended(): lax.ppermute(tail, axis, [(i, (i + 1) % count) for i in range(ends)])]
    reshape x15 -> x2, local copies, waits for them, and re-layouts: 47.4 us -> 0.12 us  [per_device(): w2 = w2.reshape(2, 14, 8, 64).transpose(0, 2, 1, 3).reshape(16, 896)]
  transfers between devices with their start and end apart: 18 -> 0, of which waited for: 3 -> 0; matrix products, arithmetic and copies ran while one was open for 12% -> 0% of each run, Pallas kernels for 0% -> 0%
where the time goes in v1:
time: 94.8 us; the launch traced here: 93.4 us
  Pallas kernels  87.9 us (93%)
  local copies, waits for them, and re-layouts  4.79 us (5%)
    pallas_call x1, Pallas kernels, per_device(): pl.pallas_call(kernel, out_shape=(jax.ShapeDtypeStruct((128, 128), BF16),...  87.9 us
    unnamed x11, local copies, waits for them, and re-layouts  3.8 us

profile of v1, /device:TPU:1, one launch (start us, length us, event | category | flops | bytes accessed | tf_op | source)
XLA Modules:
  0.0 93.4 jit_solution(8688140206298615458)
XLA Ops:
  0.6 0.0 copy-start.1
  0.6 0.9 pad.4
  1.5 0.0 copy-start.2
  1.5 0.1 reshape.23.w2_ref
  1.7 0.7 copy-done.2
  2.4 0.0 copy-done.1
  2.4 0.0 copy-start
  2.4 0.3 copy.13.w1_ref
  2.7 0.5 copy-done
  3.2 87.9 %shard_map.67 = (bf16[128,128]{1,0:T(8,128)(2,1)S(1)}, f32[27,64,32]{2,1,0:T(8,128)S(1)}, f32[27,8,64]{2,1,0:T(8,128)S(1)}) custom-call(bf16[2,32,512]{2,1,0:T(8,128)(2,1)S(1)} %bitcast.11, bf16[27,64,32]{2,1,0:T(8,128)(2,1)S(1)} %copy.13.w1_ref, bf16[16,896]{1,0:T(8,128)(2,1)S(1)} %reshape.23.w2_ref, bf16[128,128]{1,0:T(8,128)(2,1)S(1)} %bitcast.12), custom_call_target="tpu_custom_call" | custom-call | tf_op jit(solution)/shard_map/pallas_call | solution.py:434
  91.1 1.1 %copy.14 = f32[27,64,32]{1,2,0:T(8,128)} copy(f32[27,64,32]{2,1,0:T(8,128)S(1)} %get-tuple-element.13) | data formatting | bytes 442368
  92.1 0.6 copy.21
  92.7 0.6 copy.22
  (2 shorter events, 0.0 us)
Async XLA Ops:
  0.6 1.8 %copy-start.1 = (bf16[27,64,32]{1,2,0:T(8,128)(2,1)S(1)}, bf16[27,64,32]{1,2,0:T(8,128)(2,1)}, u32[]{:S(2)}) copy-start(bf16[27,64,32]{1,2,0:T(8,128)(2,1)} %param.5) | copy-start | bytes 331780
  1.5 0.8 copy-start.2
  2.4 0.8 copy-start

commit v2 on v1

v2 whole, which is shorter than its diff:
```python
import functools

import jax
import jax.numpy as jnp
from jax import lax
from jax.experimental import pallas as pl
from jax.experimental.pallas import tpu as pltpu
from jax.sharding import PartitionSpec as P

MESH = pl.DeviceIdType.MESH
BF16 = jnp.bfloat16
F32 = jnp.float32
N_SX, N_SY, N_AF = 4, 8, 16
SLOTS = [(dx, dy) for dy in (-1, 0, 1) for dx in (-1, 0, 1) if (dx, dy) != (0, 0)]


def iota(shape, axis):
    return lax.broadcasted_iota(jnp.int32, shape, axis)


def leaky(values):
    return jnp.where(values > 0, values, 0.3 * values)


def slope(values):
    return jnp.where(values > 0, 1.0, 0.3)


def one_hot(rows, source):
    return (iota((rows, source.shape[1]), 0) == source).astype(F32).astype(BF16)


def dot(a, b):
    return jnp.dot(a, b, preferred_element_type=F32)


def dot_nt(a, b):
    return lax.dot_general(a, b, (((1,), (1,)), ((), ())), preferred_element_type=F32)


def rolled(values, shift):
    shift = shift % values.shape[1]
    return values if shift == 0 else pltpu.roll(values, shift, 1)


def border_selection_one():
    lane = iota((1, 128), 1)
    source = jnp.full((1, 128), -1, jnp.int32)
    source = jnp.where(lane == 0, 511, source)
    source = jnp.where((lane >= 1) & (lane <= 16), 32 * (lane - 1) + 31, source)
    source = jnp.where(lane == 17, 31, source)
    source = jnp.where((lane >= 32) & (lane < 64), 480 + lane - 32, source)
    source = jnp.where(lane == 64, 480, source)
    source = jnp.where((lane >= 65) & (lane <= 80), 32 * (lane - 65), source)
    source = jnp.where(lane == 81, 0, source)
    source = jnp.where(lane >= 96, lane - 96, source)
    return one_hot(512, source)


def column_placement_one():
    lane = iota((1, 1536), 1)
    offset = lane // 512
    y = lane % 512 // 32
    x = lane % 32
    source = jnp.where(x == 0, y + offset, jnp.where(x == 31, 64 + y + offset, -1))
    return one_hot(128, source)


def extension():
    lane = iota((1, 256), 1)
    y, x = lane // 20 - 2, lane % 20 - 2
    dy = jnp.where(y < 0, -1, jnp.where(y >= 8, 1, 0))
    dx = jnp.where(x < 0, -1, jnp.where(x >= 16, 1, 0))
    slot = 3 * (dy + 1) + dx + 1
    slot = jnp.where(slot == 4, 8, jnp.where(slot > 4, slot - 1, slot))
    source = 128 * slot + 16 * (y - 8 * dy) + x - 16 * dx
    return one_hot(1152, jnp.where(lane < 240, source, -1))


def interior_selection():
    lane = iota((1, 128), 1)
    return one_hot(256, 20 * (lane // 16 + 2) + lane % 16 + 2)


def pool_selection():
    lane = iota((1, 128), 1)
    return one_hot(512, 64 * (lane // 16) + 2 * (lane % 16))


def spread_selection():
    lane = iota((1, 512), 1)
    return one_hot(256, 20 * (lane // 64 + 2) + lane % 32 // 2 + 2)


def kernel(
    x_ref, w1_ref, w2_ref, cot_ref,
    out_ref, grad_one_ref, grad_two_ref,
    select_one, place_one, extend, pool_select, spread_select, interior_select,
    x_all, w1_cat, w2_own, w2_all, w2_cat, w2_turned,
    pack_one, recv_one, patches_one, hidden_one,
    p_own, p_recv, p_all, patches_two, c_recv, c_all, patches_d,
    g2_send, g2_sx, g2_part, g2_af, g2_sy, g2_done,
    g1_full, g1_send, g1_sx, g1_tiles, g1_sy, g1_af, g1_part, g1_done,
    z_sems, plane_sems, w2_sems, g2_sems, g1_sems,
):
    sx, sy, af = lax.axis_index("sx"), lax.axis_index("sy"), lax.axis_index("af")
    af_x, af_y = af % 4, af // 4

    barrier = pltpu.get_barrier_semaphore()
    for axis, me, count in (("sx", sx, N_SX), ("sy", sy, N_SY), ("af", af, N_AF)):

        def greet(j, carry, axis=axis, me=me, count=count):
            pl.semaphore_signal(
                barrier, inc=1, device_id={axis: lax.rem(me + j, count)}, device_id_type=MESH
            )
            return carry

        lax.fori_loop(1, count, greet, 0)
    for dx in (1, N_SX - 1):
        for dy in (1, N_SY - 1):
            pl.semaphore_signal(
                barrier,
                inc=1,
                device_id={"sx": lax.rem(sx + dx, N_SX), "sy": lax.rem(sy + dy, N_SY)},
                device_id_type=MESH,
            )

    x_all[1] = x_ref[0]
    x_all[2] = x_ref[1]
    for t in range(7):
        rows = []
        for half in range(2):
            pair = []
            for k in (14 * half + 2 * t, 14 * half + 2 * t + 1):
                pair.append(w2_ref[k].astype(F32) if k < 27 else jnp.zeros((8, 64), F32))
            rows.append(jnp.concatenate(pair, axis=1))
        w2_own[:, 128 * t : 128 * t + 128] = jnp.concatenate(rows, axis=0).astype(BF16)
    w2_all[af_x, af_y] = w2_own[...]
    w1_cat[...] = w1_ref[...].astype(F32).reshape(864, 64).T.astype(BF16)
    select_one[...] = border_selection_one()
    place_one[...] = column_placement_one()
    extend[...] = extension()
    pool_select[...] = pool_selection()
    spread_select[...] = spread_selection()
    interior_select[...] = interior_selection()
    patches_two[2880:2944] = jnp.zeros((64, 256), BF16)

    pl.semaphore_wait(barrier, N_SX + N_SY + N_AF + 1)

    pending = []

    class Group:
        def __init__(self, count, source, target, device, sems):
            self.count = count

            def copy(j):
                return pltpu.make_async_remote_copy(
                    src_ref=source(j),
                    dst_ref=target,
                    send_sem=sems.at[0, j],
                    recv_sem=sems.at[1, j],
                    device_id=device(j),
                    device_id_type=MESH,
                )

            self.copy = copy
            self.each(lambda copy: copy.start())
            pending.append(self.wait_send)

        def each(self, act):
            def body(j, carry):
                act(self.copy(j))
                return carry

            lax.fori_loop(1, self.count, body, 0)

        def wait_recv(self):
            self.each(lambda copy: copy.wait_recv())

        def wait_send(self):
            self.each(lambda copy: copy.wait_send())

    def ring(axis, me, count, source, target, sems):
        return Group(
            count,
            lambda j: source(lax.rem(me + j, count)),
            target.at[me],
            lambda j: {axis: lax.rem(me + j, count)},
            sems,
        )

    def exchange_planes(steps, target, sems):
        copies = []
        for way, (step, source, slot) in enumerate(steps):
            copy = pltpu.make_async_remote_copy(
                src_ref=source,
                dst_ref=target.at[slot],
                send_sem=sems.at[0, way],
                recv_sem=sems.at[1, way],
                device_id={"af": lax.rem(af + N_AF + step, N_AF)},
                device_id_type=MESH,
            )
            copy.start()
            pending.append(copy.wait_send)
            copies.append(copy)
        return copies

    def exchange_borders(source, target, sems):
        copies = []
        for slot, (dx, dy) in enumerate(SLOTS):
            copy = pltpu.make_async_remote_copy(
                src_ref=source,
                dst_ref=target.at[slot],
                send_sem=sems.at[0, slot],
                recv_sem=sems.at[1, slot],
                device_id={
                    "sx": lax.rem(sx + N_SX - dx, N_SX),
                    "sy": lax.rem(sy + N_SY - dy, N_SY),
                },
                device_id_type=MESH,
            )
            copy.start()
            pending.append(copy.wait_send)
            copies.append(copy)
        return copies

    def inside(dx, dy):
        good = True
        if dx:
            good = (sx > 0) if dx < 0 else (sx < N_SX - 1)
        if dy:
            row = (sy > 0) if dy < 0 else (sy < N_SY - 1)
            good = row if good is True else good & row
        return good

    def gather_columns(received, height, right):
        first = received[0].astype(F32)
        lane = iota(first.shape, 1)
        columns = jnp.zeros(first.shape, F32)
        for dx, start in ((-1, 0), (1, right)):
            for dy, cells in (
                (0, (lane >= start + 1) & (lane <= start + height)),
                (-1, lane == start),
                (1, lane == start + height + 1),
            ):
                values = received[SLOTS.index((dx, dy))].astype(F32)
                columns = jnp.where(cells & inside(dx, dy), values, columns)
        return columns.astype(BF16)

    def masked_rows(received, dy):
        values = received[SLOTS.index((0, dy))].astype(F32)
        return jnp.where(inside(0, dy), values, 0.0)

    def extended(received, own):
        planes = []
        for slot, (dx, dy) in enumerate(SLOTS):
            planes.append(jnp.where(inside(dx, dy), received[slot].astype(F32), 0.0).astype(BF16))
        joined = jnp.concatenate(planes + [own], axis=1)
        return dot(joined, extend[...]).astype(BF16)

    x_copies = exchange_planes(
        [(-1, x_ref.at[0], 3), (1, x_ref.at[1], 0)], x_all, z_sems.at[0]
    )
    w2_far = Group(
        4,
        lambda j: w2_own,
        w2_all.at[af_x, af_y],
        lambda j: {"af": lax.rem(af_y + j, 4) * 4 + af_x},
        w2_sems.at[0],
    )
    c_copies = exchange_borders(cot_ref, c_recv, plane_sems.at[2])
    for copy in x_copies:
        copy.wait_recv()

    field = x_all[...].reshape(128, 512).astype(F32)
    row = iota((128, 512), 0)
    outer = ((row < 32) & (af == 0)) | ((row >= 96) & (af == N_AF - 1))
    field = jnp.where(outer, 0.0, field)
    pack_one[...] = dot(field.astype(BF16), select_one[...]).astype(BF16)
    copies = exchange_borders(pack_one, recv_one, plane_sems.at[0])
    w2_far.wait_recv()
    w2_near = Group(
        4,
        lambda j: w2_all.at[af_x],
        w2_all.at[af_x],
        lambda j: {"af": af_y * 4 + lax.rem(af_x + j, 4)},
        w2_sems.at[1],
    )
    for copy in c_copies:
        copy.wait_recv()
    c_all[1] = extended(c_recv, cot_ref[...])
    for copy in copies:
        copy.wait_recv()
    columns = dot(gather_columns(recv_one, 16, 64), place_one[...])
    above, below = masked_rows(recv_one, -1), masked_rows(recv_one, 1)
    lane = iota((128, 128), 1)
    x = iota((128, 512), 1) % 32
    for b in range(3):
        for c in range(3):
            dy, dx = b - 1, c - 1
            moved = rolled(field, -(32 * dy + dx))
            if dy == -1:
                first = jnp.where(lane < 32, rolled(above, -(32 + dx)), moved[:, :128])
                moved = jnp.concatenate([first, moved[:, 128:]], axis=1)
            if dy == 1:
                final = jnp.where(lane >= 96, rolled(below, -dx), moved[:, 384:])
                moved = jnp.concatenate([moved[:, :384], final], axis=1)
            if dx:
                placed = columns[:, 512 * b : 512 * b + 512]
                moved = jnp.where(x == (0 if dx < 0 else 31), placed, moved)
            moved = moved.astype(BF16)
            start = 32 * (3 * b + c)
            for z in range(4):
                patches_one[288 * z + start : 288 * z + start + 32] = moved[32 * z : 32 * z + 32]
    total = None
    for z in range(2):
        hidden = dot(w1_cat[...], patches_one[288 * z : 288 * z + 864])
        hidden_one[z] = hidden
        total = leaky(hidden) if total is None else total + leaky(hidden)
    total = total + rolled(total, -1)
    total = total + rolled(total, -32)
    p_own[...] = dot((total * 0.125).astype(BF16), pool_select[...]).astype(BF16)

    copies = exchange_borders(p_own, p_recv, plane_sems.at[1])
    c_steps = exchange_planes(
        [(-1, c_all.at[1], 2), (1, c_all.at[1], 0)], c_all, z_sems.at[2]
    )
    w2_near.wait_recv()
    pieces = [w2_all[p % 4, p // 4].astype(F32) for p in range(16)]
    for half in range(2):
        filters = jnp.concatenate([piece[8 * half : 8 * half + 8] for piece in pieces], axis=0)
        w2_cat[half] = filters.astype(BF16)
        turned = filters.T.astype(BF16)
        for place in range(14):
            k = 14 * half + place
            if k < 27:
                start = 128 * (26 - k)
                w2_turned[:, start : start + 128] = turned[64 * place : 64 * place + 64]
    for copy in copies:
        copy.wait_recv()
    p_all[2] = extended(p_recv, p_own[...])
    copies = exchange_planes(
        [(step, p_all.at[2], 2 - step) for step in (-2, -1, 1, 2)], p_all, z_sems.at[1]
    )

    def shift_plane(values, target, start, channels):
        for b in range(3):
            for c in range(3):
                moved = rolled(values, -(20 * (b - 1) + c - 1)).astype(BF16)
                place = start + channels * (3 * b + c)
                target[place : place + channels] = moved

    shift_plane(p_all[2].astype(F32), patches_two, 576 * 2, 64)
    for z, copy in ((4, copies[0]), (3, copies[1]), (1, copies[2]), (0, copies[3])):
        copy.wait_recv()
        values = p_all[z].astype(F32)
        exists = (af + z >= 2) & (af + z < N_AF + 2)
        shift_plane(jnp.where(exists, values, 0.0), patches_two, 576 * z, 64)
    for copy in c_steps:
        copy.wait_recv()

    lane = iota((128, 256), 1)
    y, x = lane // 20 - 2, lane % 20 - 2
    own = (y >= 0) & (y < 8) & (x >= 0) & (x < 16)
    grid_y, grid_x = 8 * sy + y, 16 * sx + x
    on_grid = (grid_y >= 0) & (grid_y < 8 * N_SY) & (grid_x >= 0) & (grid_x < 16 * N_SX)
    for z in range(3):
        start = 576 * z
        hidden = dot(w2_cat[0], patches_two[start : start + 896])
        hidden = hidden + dot(w2_cat[1], patches_two[start + 896 : start + 1792])
        if z == 1:
            out_ref[...] = dot(leaky(hidden).astype(BF16), interior_select[...]).astype(BF16)
        delta = (c_all[z].astype(F32) * slope(hidden)).astype(BF16).astype(F32)
        exists = (af + z >= 1) & (af + z < N_AF + 1)
        delta = jnp.where(on_grid & exists, delta, 0.0)
        if z == 1:
            delta_two = jnp.where(own, delta, 0.0).astype(BF16)
        shift_plane(delta, patches_d, 1152 * z, 128)

    halves = []
    for half in range(2):
        start = 576 + 896 * half
        part = dot_nt(delta_two, patches_two[start : start + 896]).reshape(16, 1, 8, 896)
        halves.append(part)
    parts = jnp.concatenate(halves, axis=1).reshape(16, 16, 896).astype(BF16)
    for q in range(3):
        g2_send[q] = parts[:, :, 256 * q : 256 * q + 256]
    g2_send[3] = jnp.concatenate([parts[:, :, 768:], jnp.zeros((16, 16, 128), BF16)], axis=2)
    g2_sx_ring = ring("sx", sx, N_SX, lambda peer: g2_send.at[peer], g2_sx, g2_sems.at[0])
    g2_sx[sx] = g2_send[sx]

    pooled_grad = dot(w2_turned[...], patches_d[...]).astype(BF16)

    spread = dot(pooled_grad, spread_select[...]) * 0.125
    total = None
    for z in range(2):
        delta_one = (spread * slope(hidden_one[z])).astype(BF16)
        part = dot_nt(delta_one, patches_one[288 * z : 288 * z + 864])
        total = part if total is None else total + part
    g1_full[:, 768:] = jnp.zeros((64, 128), F32)
    g1_full[:, :864] = total
    g1_send[...] = g1_full[...].astype(BF16).reshape(4, 16, 896)
    g1_sx_ring = ring("sx", sx, N_SX, lambda peer: g1_send.at[peer], g1_sx, g1_sems.at[0])
    g1_sx[sx] = g1_send[sx]

    g2_sx_ring.wait_recv()
    g2_part[...] = jnp.sum(g2_sx[...].astype(F32), axis=0).astype(BF16)
    g2_af_ring = ring("af", af, N_AF, lambda peer: g2_part.at[peer], g2_af, g2_sems.at[1])
    g2_af[af] = g2_part[af]

    g1_sx_ring.wait_recv()
    sums = jnp.sum(g1_sx[...].astype(F32), axis=0).astype(BF16)
    for t in range(7):
        g1_tiles[t] = sums[:, 128 * t : 128 * t + 128]
    g1_tiles[7] = jnp.zeros((16, 128), BF16)
    g1_sy_ring = ring("sy", sy, N_SY, lambda peer: g1_tiles.at[peer], g1_sy, g1_sems.at[1])
    g1_sy[sy] = g1_tiles[sy]

    g1_sy_ring.wait_recv()
    g1_af[af] = jnp.sum(g1_sy[...].astype(F32), axis=0).astype(BF16)
    g1_af_ring = ring("af", af, N_AF, lambda peer: g1_af.at[af], g1_af, g1_sems.at[2])

    g2_af_ring.wait_recv()
    g2_sy[sy] = jnp.sum(g2_af[...].astype(F32), axis=0).astype(BF16)
    g2_sy_ring = ring("sy", sy, N_SY, lambda peer: g2_sy.at[sy], g2_sy, g2_sems.at[2])

    g1_af_ring.wait_recv()
    sums = jnp.sum(g1_af[...].astype(F32), axis=0) * (524288.0**-0.5)
    g1_part[sy] = sums.astype(BF16)
    g1_part_ring = ring("sy", sy, N_SY, lambda peer: g1_part.at[sy], g1_part, g1_sems.at[3])

    g2_sy_ring.wait_recv()
    sums = jnp.sum(g2_sy[...].astype(F32), axis=0) * (1.0 / 256.0)
    g2_done[sx] = sums.astype(BF16)
    g2_done_ring = ring("sx", sx, N_SX, lambda peer: g2_done.at[sx], g2_done, g2_sems.at[3])

    g1_part_ring.wait_recv()
    g1_done_ring = ring("sx", sx, N_SX, lambda peer: g1_part, g1_done, g1_sems.at[4])
    g1_done[sx] = g1_part[...]

    g2_done_ring.wait_recv()
    for k in range(27):
        half, place = k // 14, k % 14
        tile = g2_done[place // 4].astype(F32)[8 * half : 8 * half + 8]
        grad_two_ref[k] = tile[:, 64 * (place % 4) : 64 * (place % 4) + 64]

    g1_done_ring.wait_recv()
    for t in range(7):
        tile = jnp.concatenate([g1_done[q, t].astype(F32) for q in range(4)], axis=0).T
        for k in range(4 * t, min(4 * t + 4, 27)):
            grad_one_ref[k] = tile[32 * (k - 4 * t) : 32 * (k - 4 * t) + 32]

    for wait in pending:
        wait()


def per_device(inputs, weight_one, weight_two, cotangent):
    x = inputs.reshape(32, 2, 512).transpose(1, 0, 2)
    cot = cotangent.reshape(128, 128)
    vmem = pl.BlockSpec(memory_space=pltpu.VMEM)
    output, grad_one, grad_two = pl.pallas_call(
        kernel,
        out_shape=(
            jax.ShapeDtypeStruct((128, 128), BF16),
            jax.ShapeDtypeStruct((27, 32, 64), F32),
            jax.ShapeDtypeStruct((27, 8, 64), F32),
        ),
        in_specs=[vmem] * 4,
        out_specs=(vmem, vmem, vmem),
        scratch_shapes=[
            pltpu.VMEM((512, 128), BF16),
            pltpu.VMEM((128, 1536), BF16),
            pltpu.VMEM((1152, 256), BF16),
            pltpu.VMEM((512, 128), BF16),
            pltpu.VMEM((256, 512), BF16),
            pltpu.VMEM((256, 128), BF16),
            pltpu.VMEM((4, 32, 512), BF16),
            pltpu.VMEM((64, 864), BF16),
            pltpu.VMEM((16, 896), BF16),
            pltpu.VMEM((4, 4, 16, 896), BF16),
            pltpu.VMEM((2, 128, 896), BF16),
            pltpu.VMEM((64, 3456), BF16),
            pltpu.VMEM((128, 128), BF16),
            pltpu.VMEM((8, 128, 128), BF16),
            pltpu.VMEM((1152, 512), BF16),
            pltpu.VMEM((2, 64, 512), F32),
            pltpu.VMEM((64, 128), BF16),
            pltpu.VMEM((8, 64, 128), BF16),
            pltpu.VMEM((5, 64, 256), BF16),
            pltpu.VMEM((2944, 256), BF16),
            pltpu.VMEM((8, 128, 128), BF16),
            pltpu.VMEM((3, 128, 256), BF16),
            pltpu.VMEM((3456, 256), BF16),
            pltpu.VMEM((4, 16, 16, 256), BF16),
            pltpu.VMEM((4, 16, 16, 256), BF16),
            pltpu.VMEM((16, 16, 256), BF16),
            pltpu.VMEM((16, 16, 256), BF16),
            pltpu.VMEM((8, 16, 256), BF16),
            pltpu.VMEM((4, 16, 256), BF16),
            pltpu.VMEM((64, 896), F32),
            pltpu.VMEM((4, 16, 896), BF16),
            pltpu.VMEM((4, 16, 896), BF16),
            pltpu.VMEM((8, 16, 128), BF16),
            pltpu.VMEM((8, 16, 128), BF16),
            pltpu.VMEM((16, 16, 128), BF16),
            pltpu.VMEM((8, 16, 128), BF16),
            pltpu.VMEM((4, 8, 16, 128), BF16),
            pltpu.SemaphoreType.DMA((3, 2, 4)),
            pltpu.SemaphoreType.DMA((3, 2, 8)),
            pltpu.SemaphoreType.DMA((2, 2, 4)),
            pltpu.SemaphoreType.DMA((4, 2, 16)),
            pltpu.SemaphoreType.DMA((5, 2, 16)),
        ],
        compiler_params=pltpu.CompilerParams(
            collective_id=0, has_side_effects=True, vmem_limit_bytes=48 * 2**20
        ),
    )(x, weight_one.transpose(0, 2, 1), weight_two, cot)
    return output.reshape(128, 1, 1, 1, 128), grad_one.transpose(0, 2, 1), grad_two


def solution(mesh):
    placed = (
        P(None, "af", "sy", "sx", None),
        P(),
        P(None, "af", None),
        P(None, "af", "sy", "sx", None),
    )
    return jax.shard_map(
        per_device,
        mesh=mesh,
        in_specs=placed,
        out_specs=(P(None, "af", "sy", "sx", None), P(), P(None, "af", None)),
        check_vma=False,
    )
```

time: 94.8 us -> 76.6 us (0.81); the launches traced: 93.4 us -> 76.4 us
  Pallas kernels: 87.9 us -> 71.9 us
  local copies, waits for them, and re-layouts: 4.79 us -> 3.83 us
    pallas_call x1, Pallas kernels: 87.9 us -> 71.9 us  [per_device(): pl.pallas_call(kernel, out_shape=(jax.ShapeDtypeStruct((128, 128), BF16),...]
    unnamed x11 -> x10, local copies, waits for them, and re-layouts: 3.8 us -> 3.83 us
where the time goes in v2:
time: 76.6 us; the launch traced here: 76.4 us
  Pallas kernels  71.9 us (94%)
  local copies, waits for them, and re-layouts  3.83 us (5%)
    pallas_call x1, Pallas kernels, per_device(): pl.pallas_call(kernel, out_shape=(jax.ShapeDtypeStruct((128, 128), BF16),...  71.9 us
    unnamed x10, local copies, waits for them, and re-layouts  3.83 us

profile of v2, /device:TPU:1, one launch (start us, length us, event | category | flops | bytes accessed | tf_op | source)
XLA Modules:
  0.0 76.4 jit_solution(6966718474597894603)
XLA Ops:
  0.6 0.0 copy-start.1
  0.6 0.0 copy-start.2
  0.7 0.9 %copy.9 = bf16[32,2,1,1,512]{4,0,1,3,2:T(8,128)(2,1)S(1)} copy(bf16[32,2,1,1,512]{4,1,3,2,0:T(2,128)(2,1)} %param.4) | data formatting | bytes 131072 | tf_op args[0]
  1.5 0.0 copy-done.1
  1.5 0.0 copy-done.2
  1.5 0.0 copy-start
  1.6 0.9 %copy-done = bf16[27,64,32]{1,2,0:T(8,128)(2,1)S(1)} copy-done((bf16[27,64,32]{1,2,0:T(8,128)(2,1)S(1)}, bf16[27,64,32]{1,2,0:T(8,128)(2,1)}, u32[]{:S(2)}) %copy-start) | copy-done | bytes 110616
  2.5 71.9 %shard_map.67 = (bf16[128,128]{1,0:T(8,128)(2,1)S(1)}, f32[27,32,64]{2,1,0:T(8,128)S(1)}, f32[27,8,64]{2,1,0:T(8,128)S(1)}) custom-call(bf16[2,32,512]{2,1,0:T(8,128)(2,1)S(1)} %bitcast.10, bf16[27,32,64]{2,1,0:T(8,128)(2,1)S(1)} %bitcast.11, bf16[27,8,64]{2,1,0:T(8,128)(2,1)S(1)} %copy-done.1, bf16[128,128]{1,0:T(8,128)(2,1)S(1)} %bitcast.12), custom_call_target="tpu_custom_call" | custom-call | tf_op jit(solution)/shard_map/pallas_call | solution.py:461
  74.4 0.6 copy.13
  75.0 0.8 copy.14
  75.8 0.6 copy.15
Async XLA Ops:
  0.6 0.9 %copy-start.1 = (bf16[27,8,64]{2,1,0:T(8,128)(2,1)S(1)}, bf16[27,8,64]{2,1,0:T(8,128)(2,1)}, u32[]{:S(2)}) copy-start(bf16[27,8,64]{2,1,0:T(8,128)(2,1)} %w2_ref.1) | copy-start | bytes 82948
  0.6 0.9 %copy-start.2 = (bf16[128,1,1,1,128]{4,0,3,2,1:T(8,128)(2,1)S(1)}, bf16[128,1,1,1,128]{4,0,3,2,1:T(8,128)(2,1)}, u32[]{:S(2)}) copy-start(bf16[128,1,1,1,128]{4,0,3,2,1:T(8,128)(2,1)} %param.7) | copy-start | bytes 98308
  1.5 0.9 %copy-start = (bf16[27,64,32]{1,2,0:T(8,128)(2,1)S(1)}, bf16[27,64,32]{1,2,0:T(8,128)(2,1)}, u32[]{:S(2)}) copy-start(bf16[27,64,32]{1,2,0:T(8,128)(2,1)} %param.5) | copy-start | bytes 331780

commit v3 on v2

--- a/solution.py
+++ b/solution.py
@@ -99,34 +99,28 @@
     x_all, w1_cat, w2_own, w2_all, w2_cat, w2_turned,
     pack_one, recv_one, patches_one, hidden_one,
     p_own, p_recv, p_all, patches_two, c_recv, c_all, patches_d,
-    g2_send, g2_sx, g2_part, g2_af, g2_sy, g2_done,
-    g1_full, g1_send, g1_sx, g1_tiles, g1_sy, g1_af, g1_part, g1_done,
+    g2_send, g2_pair, g2_part, g2_recv, g2_tiles, g2_far, g2_sy, g2_done,
+    g1_full, g1_send, g1_recv, g1_far, g1_sy, g1_done,
     z_sems, plane_sems, w2_sems, g2_sems, g1_sems,
 ):
     sx, sy, af = lax.axis_index("sx"), lax.axis_index("sy"), lax.axis_index("af")
     af_x, af_y = af % 4, af // 4
+    core, half_y = sx % 2, sx // 2
 
     barrier = pltpu.get_barrier_semaphore()
-    for axis, me, count in (("sx", sx, N_SX), ("sy", sy, N_SY), ("af", af, N_AF)):
-
-        def greet(j, carry, axis=axis, me=me, count=count):
-            pl.semaphore_signal(
-                barrier, inc=1, device_id={axis: lax.rem(me + j, count)}, device_id_type=MESH
-            )
-            return carry
-
-        lax.fori_loop(1, count, greet, 0)
-    for dx in (1, N_SX - 1):
-        for dy in (1, N_SY - 1):
-            pl.semaphore_signal(
-                barrier,
-                inc=1,
-                device_id={"sx": lax.rem(sx + dx, N_SX), "sy": lax.rem(sy + dy, N_SY)},
-                device_id_type=MESH,
-            )
-
-    x_all[1] = x_ref[0]
-    x_all[2] = x_ref[1]
+    greeted = [
+        {"sx": lax.rem(sx + dx, N_SX), "sy": lax.rem(sy + dy, N_SY)}
+        for dx in (0, 1, N_SX - 1)
+        for dy in (0, 1, N_SY - 1)
+        if dx or dy
+    ]
+    greeted += [{"af": lax.rem(af + step, N_AF)} for step in (1, N_AF - 1)]
+    greeted += [{"af": af_y * 4 + lax.rem(af_x + j, 4)} for j in (1, 2, 3)]
+    greeted += [{"af": lax.rem(af_y + j, 4) * 4 + af_x} for j in (1, 2, 3)]
+    greeted += [{"sy": lax.rem(sy + N_SY // 2, N_SY)}]
+    for device in greeted:
+        pl.semaphore_signal(barrier, inc=1, device_id=device, device_id_type=MESH)
+
     for t in range(7):
         rows = []
         for half in range(2):
@@ -135,17 +129,7 @@
                 pair.append(w2_ref[k].astype(F32) if k < 27 else jnp.zeros((8, 64), F32))
             rows.append(jnp.concatenate(pair, axis=1))
         w2_own[:, 128 * t : 128 * t + 128] = jnp.concatenate(rows, axis=0).astype(BF16)
-    w2_all[af_x, af_y] = w2_own[...]
-    w1_cat[...] = w1_ref[...].astype(F32).reshape(864, 64).T.astype(BF16)
-    select_one[...] = border_selection_one()
-    place_one[...] = column_placement_one()
-    extend[...] = extension()
-    pool_select[...] = pool_selection()
-    spread_select[...] = spread_selection()
-    interior_select[...] = interior_selection()
-    patches_two[2880:2944] = jnp.zeros((64, 256), BF16)
-
-    pl.semaphore_wait(barrier, N_SX + N_SY + N_AF + 1)
+    pl.semaphore_wait(barrier, len(greeted))
 
     pending = []
 
@@ -269,6 +253,18 @@
         w2_sems.at[0],
     )
     c_copies = exchange_borders(cot_ref, c_recv, plane_sems.at[2])
+
+    x_all[1] = x_ref[0]
+    x_all[2] = x_ref[1]
+    w2_all[af_x, af_y] = w2_own[...]
+    select_one[...] = border_selection_one()
+    place_one[...] = column_placement_one()
+    w1_cat[...] = w1_ref[...].astype(F32).reshape(864, 64).T.astype(BF16)
+    extend[...] = extension()
+    pool_select[...] = pool_selection()
+    spread_select[...] = spread_selection()
+    interior_select[...] = interior_selection()
+    patches_two[2880:2944] = jnp.zeros((64, 256), BF16)
     for copy in x_copies:
         copy.wait_recv()
 
@@ -383,11 +379,17 @@
         part = dot_nt(delta_two, patches_two[start : start + 896]).reshape(16, 1, 8, 896)
         halves.append(part)
     parts = jnp.concatenate(halves, axis=1).reshape(16, 16, 896).astype(BF16)
-    for q in range(3):
-        g2_send[q] = parts[:, :, 256 * q : 256 * q + 256]
-    g2_send[3] = jnp.concatenate([parts[:, :, 768:], jnp.zeros((16, 16, 128), BF16)], axis=2)
-    g2_sx_ring = ring("sx", sx, N_SX, lambda peer: g2_send.at[peer], g2_sx, g2_sems.at[0])
-    g2_sx[sx] = g2_send[sx]
+    parts = jnp.concatenate([parts, jnp.zeros((16, 16, 128), BF16)], axis=2)
+    for p in range(16):
+        for q in range(4):
+            g2_send[q % 2, q // 2, p % 4, p // 4] = parts[p][:, 256 * q : 256 * q + 256]
+    g2_core = Group(
+        2,
+        lambda j: g2_send.at[1 - core],
+        g2_pair,
+        lambda j: {"sx": sx + 1 - 2 * core},
+        g2_sems.at[0],
+    )
 
     pooled_grad = dot(w2_turned[...], patches_d[...]).astype(BF16)
 
@@ -397,56 +399,95 @@
         delta_one = (spread * slope(hidden_one[z])).astype(BF16)
         part = dot_nt(delta_one, patches_one[288 * z : 288 * z + 864])
         total = part if total is None else total + part
-    g1_full[:, 768:] = jnp.zeros((64, 128), F32)
+    g1_full[:, 768:] = jnp.zeros((64, 256), F32)
     g1_full[:, :864] = total
-    g1_send[...] = g1_full[...].astype(BF16).reshape(4, 16, 896)
-    g1_sx_ring = ring("sx", sx, N_SX, lambda peer: g1_send.at[peer], g1_sx, g1_sems.at[0])
-    g1_sx[sx] = g1_send[sx]
-
-    g2_sx_ring.wait_recv()
-    g2_part[...] = jnp.sum(g2_sx[...].astype(F32), axis=0).astype(BF16)
-    g2_af_ring = ring("af", af, N_AF, lambda peer: g2_part.at[peer], g2_af, g2_sems.at[1])
-    g2_af[af] = g2_part[af]
-
-    g1_sx_ring.wait_recv()
-    sums = jnp.sum(g1_sx[...].astype(F32), axis=0).astype(BF16)
-    for t in range(7):
-        g1_tiles[t] = sums[:, 128 * t : 128 * t + 128]
-    g1_tiles[7] = jnp.zeros((16, 128), BF16)
-    g1_sy_ring = ring("sy", sy, N_SY, lambda peer: g1_tiles.at[peer], g1_sy, g1_sems.at[1])
-    g1_sy[sy] = g1_tiles[sy]
+    sums = g1_full[...].astype(BF16)
+    for q in range(4):
+        for t in range(4):
+            g1_send[q, t] = sums[16 * q : 16 * q + 16, 256 * t : 256 * t + 256]
+
+    def near(j):
+        return lax.rem(sx + j // 4, N_SX), lax.rem(af_x + j % 4, 4)
+
+    def near_device(j):
+        return {"sx": near(j)[0], "af": af_y * 4 + near(j)[1]}
+
+    def far_device(j):
+        return {"af": lax.rem(af_y + j, 4) * 4 + af_x}
+
+    g1_near = Group(16, lambda j: g1_send.at[near(j)], g1_recv.at[sx, af_x], near_device, g1_sems.at[0])
+    g1_recv[sx, af_x] = g1_send[sx, af_x]
+
+    g2_core.wait_recv()
+    mine = g2_send[core].astype(F32) + g2_pair[...].astype(F32)
+    g2_part[...] = mine.astype(BF16)
+
+    def beside(j):
+        return lax.rem(half_y + j // 4, 2), lax.rem(af_x + j % 4, 4)
+
+    g2_near = Group(
+        8,
+        lambda j: g2_part.at[beside(j)],
+        g2_recv.at[half_y, af_x],
+        lambda j: {"sx": beside(j)[0] * 2 + core, "af": af_y * 4 + beside(j)[1]},
+        g2_sems.at[1],
+    )
+    g2_recv[half_y, af_x] = g2_part[half_y, af_x]
+
+    g1_near.wait_recv()
+    g1_far[af_y] = jnp.sum(g1_recv[...].astype(F32).reshape(16, 16, 256), axis=0).astype(BF16)
+    g1_far_group = Group(4, lambda j: g1_far.at[af_y], g1_far.at[af_y], far_device, g1_sems.at[1])
+
+    g2_near.wait_recv()
+    sums = jnp.sum(g2_recv[...].astype(F32).reshape(8, 4, 16, 256), axis=0)
+    g2_tiles[...] = sums.astype(BF16)
+    g2_far_group = Group(
+        4,
+        lambda j: g2_tiles.at[lax.rem(af_y + j, 4)],
+        g2_far.at[af_y],
+        far_device,
+        g2_sems.at[2],
+    )
+    g2_far[af_y] = g2_tiles[af_y]
+
+    g1_far_group.wait_recv()
+    g1_sy[sy] = jnp.sum(g1_far[...].astype(F32), axis=0).astype(BF16)
+    g1_sy_ring = ring("sy", sy, N_SY, lambda peer: g1_sy.at[sy], g1_sy, g1_sems.at[2])
+
+    g2_far_group.wait_recv()
+    g2_sy[sy] = jnp.sum(g2_far[...].astype(F32), axis=0).astype(BF16)
+    g2_sy_ring = ring("sy", sy, N_SY, lambda peer: g2_sy.at[sy], g2_sy, g2_sems.at[3])
 
     g1_sy_ring.wait_recv()
-    g1_af[af] = jnp.sum(g1_sy[...].astype(F32), axis=0).astype(BF16)
-    g1_af_ring = ring("af", af, N_AF, lambda peer: g1_af.at[af], g1_af, g1_sems.at[2])
-
-    g2_af_ring.wait_recv()
-    g2_sy[sy] = jnp.sum(g2_af[...].astype(F32), axis=0).astype(BF16)
-    g2_sy_ring = ring("sy", sy, N_SY, lambda peer: g2_sy.at[sy], g2_sy, g2_sems.at[2])
-
-    g1_af_ring.wait_recv()
-    sums = jnp.sum(g1_af[...].astype(F32), axis=0) * (524288.0**-0.5)
-    g1_part[sy] = sums.astype(BF16)
-    g1_part_ring = ring("sy", sy, N_SY, lambda peer: g1_part.at[sy], g1_part, g1_sems.at[3])
+    sums = jnp.sum(g1_sy[...].astype(F32), axis=0) * (524288.0**-0.5)
+    g1_done[sx, af_x] = sums.astype(BF16)
+    g1_done_group = Group(
+        16,
+        lambda j: g1_done.at[sx, af_x],
+        g1_done.at[sx, af_x],
+        near_device,
+        g1_sems.at[3],
+    )
 
     g2_sy_ring.wait_recv()
     sums = jnp.sum(g2_sy[...].astype(F32), axis=0) * (1.0 / 256.0)
     g2_done[sx] = sums.astype(BF16)
-    g2_done_ring = ring("sx", sx, N_SX, lambda peer: g2_done.at[sx], g2_done, g2_sems.at[3])
-
-    g1_part_ring.wait_recv()
-    g1_done_ring = ring("sx", sx, N_SX, lambda peer: g1_part, g1_done, g1_sems.at[4])
-    g1_done[sx] = g1_part[...]
+    g2_done_ring = ring("sx", sx, N_SX, lambda peer: g2_done.at[sx], g2_done, g2_sems.at[4])
 
     g2_done_ring.wait_recv()
     for k in range(27):
         half, place = k // 14, k % 14
-        tile = g2_done[place // 4].astype(F32)[8 * half : 8 * half + 8]
+        q = place // 4
+        tile = g2_done[q].astype(F32)[8 * half : 8 * half + 8]
         grad_two_ref[k] = tile[:, 64 * (place % 4) : 64 * (place % 4) + 64]
 
-    g1_done_ring.wait_recv()
+    g1_done_group.wait_recv()
     for t in range(7):
-        tile = jnp.concatenate([g1_done[q, t].astype(F32) for q in range(4)], axis=0).T
+        rows = [
+            g1_done[q, t // 2].astype(F32)[:, 128 * (t % 2) : 128 * (t % 2) + 128]
+            for q in range(4)
+        ]
+        tile = jnp.concatenate(rows, axis=0).T
         for k in range(4 * t, min(4 * t + 4, 27)):
             grad_one_ref[k] = tile[32 * (k - 4 * t) : 32 * (k - 4 * t) + 32]
 
@@ -491,25 +532,25 @@
             pltpu.VMEM((8, 128, 128), BF16),
             pltpu.VMEM((3, 128, 256), BF16),
             pltpu.VMEM((3456, 256), BF16),
-            pltpu.VMEM((4, 16, 16, 256), BF16),
-            pltpu.VMEM((4, 16, 16, 256), BF16),
-            pltpu.VMEM((16, 16, 256), BF16),
-            pltpu.VMEM((16, 16, 256), BF16),
+            pltpu.VMEM((2, 2, 4, 4, 16, 256), BF16),
+            pltpu.VMEM((2, 4, 4, 16, 256), BF16),
+            pltpu.VMEM((2, 4, 4, 16, 256), BF16),
+            pltpu.VMEM((2, 4, 4, 16, 256), BF16),
+            pltpu.VMEM((4, 16, 256), BF16),
+            pltpu.VMEM((4, 16, 256), BF16),
             pltpu.VMEM((8, 16, 256), BF16),
             pltpu.VMEM((4, 16, 256), BF16),
-            pltpu.VMEM((64, 896), F32),
-            pltpu.VMEM((4, 16, 896), BF16),
-            pltpu.VMEM((4, 16, 896), BF16),
-            pltpu.VMEM((8, 16, 128), BF16),
-            pltpu.VMEM((8, 16, 128), BF16),
-            pltpu.VMEM((16, 16, 128), BF16),
-            pltpu.VMEM((8, 16, 128), BF16),
-            pltpu.VMEM((4, 8, 16, 128), BF16),
+            pltpu.VMEM((64, 1024), F32),
+            pltpu.VMEM((4, 4, 16, 256), BF16),
+            pltpu.VMEM((4, 4, 16, 256), BF16),
+            pltpu.VMEM((4, 16, 256), BF16),
+            pltpu.VMEM((8, 16, 256), BF16),
+            pltpu.VMEM((4, 4, 16, 256), BF16),
             pltpu.SemaphoreType.DMA((3, 2, 4)),
             pltpu.SemaphoreType.DMA((3, 2, 8)),
             pltpu.SemaphoreType.DMA((2, 2, 4)),
+            pltpu.SemaphoreType.DMA((5, 2, 8)),
             pltpu.SemaphoreType.DMA((4, 2, 16)),
-            pltpu.SemaphoreType.DMA((5, 2, 16)),
         ],
         compiler_params=pltpu.CompilerParams(
             collective_id=0, has_side_effects=True, vmem_limit_bytes=48 * 2**20

time: 76.6 us -> 67 us (0.87)
  Pallas kernels: 71.9 us -> 62.3 us
    pallas_call x1, Pallas kernels: 71.9 us -> 62.3 us  [per_device(): pl.pallas_call(kernel, out_shape=(jax.ShapeDtypeStruct((128, 128), BF16),...]
where the time goes in v3:
time: 67 us; the launch traced here: 66.8 us
  Pallas kernels  62.3 us (93%)
  local copies, waits for them, and re-layouts  3.83 us (6%)
  between operations  0.68 us (1%)
    pallas_call x1, Pallas kernels, per_device(): pl.pallas_call(kernel, out_shape=(jax.ShapeDtypeStruct((128, 128), BF16),...  62.3 us
    unnamed x10, local copies, waits for them, and re-layouts  3.83 us

profile of v3, /device:TPU:1, one launch (start us, length us, event | category | flops | bytes accessed | tf_op | source)
XLA Modules:
  0.0 66.8 jit_solution(8323682140260903292)
XLA Ops:
  0.6 0.0 copy-start.1
  0.6 0.0 copy-start.2
  0.7 0.9 %copy.9 = bf16[32,2,1,1,512]{4,0,1,3,2:T(8,128)(2,1)S(1)} copy(bf16[32,2,1,1,512]{4,1,3,2,0:T(2,128)(2,1)} %param.4) | data formatting | bytes 131072 | tf_op args[0]
  1.5 0.0 copy-done.1
  1.5 0.0 copy-done.2
  1.5 0.0 copy-start
  1.6 0.9 %copy-done = bf16[27,64,32]{1,2,0:T(8,128)(2,1)S(1)} copy-done((bf16[27,64,32]{1,2,0:T(8,128)(2,1)S(1)}, bf16[27,64,32]{1,2,0:T(8,128)(2,1)}, u32[]{:S(2)}) %copy-start) | copy-done | bytes 110616
  2.5 62.3 %shard_map.67 = (bf16[128,128]{1,0:T(8,128)(2,1)S(1)}, f32[27,32,64]{2,1,0:T(8,128)S(1)}, f32[27,8,64]{2,1,0:T(8,128)S(1)}) custom-call(bf16[2,32,512]{2,1,0:T(8,128)(2,1)S(1)} %bitcast.10, bf16[27,32,64]{2,1,0:T(8,128)(2,1)S(1)} %bitcast.11, bf16[27,8,64]{2,1,0:T(8,128)(2,1)S(1)} %copy-done.1, bf16[128,128]{1,0:T(8,128)(2,1)S(1)} %bitcast.12), custom_call_target="tpu_custom_call" | custom-call | tf_op jit(solution)/shard_map/pallas_call | solution.py:502
  64.8 0.6 copy.13
  65.4 0.8 %copy.14 = f32[27,64,32]{1,2,0:T(8,128)} copy(f32[27,64,32]{1,2,0:T(8,128)S(1)} %bitcast.9) | data formatting | bytes 442368
  66.1 0.6 copy.15
Async XLA Ops:
  0.6 0.9 %copy-start.1 = (bf16[27,8,64]{2,1,0:T(8,128)(2,1)S(1)}, bf16[27,8,64]{2,1,0:T(8,128)(2,1)}, u32[]{:S(2)}) copy-start(bf16[27,8,64]{2,1,0:T(8,128)(2,1)} %w2_ref.1) | copy-start | bytes 82948
  0.6 0.9 %copy-start.2 = (bf16[128,1,1,1,128]{4,0,3,2,1:T(8,128)(2,1)S(1)}, bf16[128,1,1,1,128]{4,0,3,2,1:T(8,128)(2,1)}, u32[]{:S(2)}) copy-start(bf16[128,1,1,1,128]{4,0,3,2,1:T(8,128)(2,1)} %param.7) | copy-start | bytes 98308
  1.5 0.9 %copy-start = (bf16[27,64,32]{1,2,0:T(8,128)(2,1)S(1)}, bf16[27,64,32]{1,2,0:T(8,128)(2,1)}, u32[]{:S(2)}) copy-start(bf16[27,64,32]{1,2,0:T(8,128)(2,1)} %param.5) | copy-start | bytes 331780

commit v4 on v3

--- a/solution.py
+++ b/solution.py
@@ -94,13 +94,13 @@
 
 def kernel(
     x_ref, w1_ref, w2_ref, cot_ref,
-    out_ref, grad_one_ref, grad_two_ref,
+    out_ref, one_ref, two_ref,
     select_one, place_one, extend, pool_select, spread_select, interior_select,
     x_all, w1_cat, w2_own, w2_all, w2_cat, w2_turned,
     pack_one, recv_one, patches_one, hidden_one,
     p_own, p_recv, p_all, patches_two, c_recv, c_all, patches_d,
-    g2_send, g2_pair, g2_part, g2_recv, g2_tiles, g2_far, g2_sy, g2_done,
-    g1_full, g1_send, g1_recv, g1_far, g1_sy, g1_done,
+    g2_send, g2_pair, g2_part, g2_recv, g2_tiles, g2_far, g2_done,
+    g1_send, g1_recv, g1_far, g1_done, both,
     z_sems, plane_sems, w2_sems, g2_sems, g1_sems,
 ):
     sx, sy, af = lax.axis_index("sx"), lax.axis_index("sy"), lax.axis_index("af")
@@ -121,6 +121,9 @@
     for device in greeted:
         pl.semaphore_signal(barrier, inc=1, device_id=device, device_id_type=MESH)
 
+    x_raw = x_ref[...].astype(F32)
+    x_all[1] = x_raw[:, 0].astype(BF16)
+    x_all[2] = x_raw[:, 1].astype(BF16)
     for t in range(7):
         rows = []
         for half in range(2):
@@ -152,11 +155,8 @@
             pending.append(self.wait_send)
 
         def each(self, act):
-            def body(j, carry):
+            for j in range(1, self.count):
                 act(self.copy(j))
-                return carry
-
-            lax.fori_loop(1, self.count, body, 0)
 
         def wait_recv(self):
             self.each(lambda copy: copy.wait_recv())
@@ -243,7 +243,7 @@
         return dot(joined, extend[...]).astype(BF16)
 
     x_copies = exchange_planes(
-        [(-1, x_ref.at[0], 3), (1, x_ref.at[1], 0)], x_all, z_sems.at[0]
+        [(-1, x_all.at[1], 3), (1, x_all.at[2], 0)], x_all, z_sems.at[0]
     )
     w2_far = Group(
         4,
@@ -254,8 +254,6 @@
     )
     c_copies = exchange_borders(cot_ref, c_recv, plane_sems.at[2])
 
-    x_all[1] = x_ref[0]
-    x_all[2] = x_ref[1]
     w2_all[af_x, af_y] = w2_own[...]
     select_one[...] = border_selection_one()
     place_one[...] = column_placement_one()
@@ -396,15 +394,12 @@
     spread = dot(pooled_grad, spread_select[...]) * 0.125
     total = None
     for z in range(2):
-        delta_one = (spread * slope(hidden_one[z])).astype(BF16)
-        part = dot_nt(delta_one, patches_one[288 * z : 288 * z + 864])
+        delta_one = (spread * slope(hidden_one[z])).T.astype(BF16)
+        part = dot(patches_one[288 * z : 288 * z + 864], delta_one)
         total = part if total is None else total + part
-    g1_full[:, 768:] = jnp.zeros((64, 256), F32)
-    g1_full[:, :864] = total
-    sums = g1_full[...].astype(BF16)
-    for q in range(4):
-        for t in range(4):
-            g1_send[q, t] = sums[16 * q : 16 * q + 16, 256 * t : 256 * t + 256]
+    rest = jnp.concatenate([total[512:], jnp.zeros((160, 64), F32)], axis=0)
+    sums = jnp.concatenate([total[:512], rest], axis=1).astype(BF16)
+    g1_send[...] = sums.reshape(4, 4, 32, 128)
 
     def near(j):
         return lax.rem(sx + j // 4, N_SX), lax.rem(af_x + j % 4, 4)
@@ -435,7 +430,7 @@
     g2_recv[half_y, af_x] = g2_part[half_y, af_x]
 
     g1_near.wait_recv()
-    g1_far[af_y] = jnp.sum(g1_recv[...].astype(F32).reshape(16, 16, 256), axis=0).astype(BF16)
+    g1_far[af_y] = jnp.sum(g1_recv[...].astype(F32).reshape(16, 32, 128), axis=0).astype(BF16)
     g1_far_group = Group(4, lambda j: g1_far.at[af_y], g1_far.at[af_y], far_device, g1_sems.at[1])
 
     g2_near.wait_recv()
@@ -451,60 +446,61 @@
     g2_far[af_y] = g2_tiles[af_y]
 
     g1_far_group.wait_recv()
-    g1_sy[sy] = jnp.sum(g1_far[...].astype(F32), axis=0).astype(BF16)
-    g1_sy_ring = ring("sy", sy, N_SY, lambda peer: g1_sy.at[sy], g1_sy, g1_sems.at[2])
-
+    both[sy, 0] = jnp.sum(g1_far[...].astype(F32), axis=0).astype(BF16)
+
+    def along_sy(j):
+        return {"sy": lax.rem(sy + j, N_SY)}
+
+    g1_sy_group = Group(N_SY, lambda j: both.at[sy, 0], both.at[sy, 0], along_sy, g1_sems.at[3])
     g2_far_group.wait_recv()
-    g2_sy[sy] = jnp.sum(g2_far[...].astype(F32), axis=0).astype(BF16)
-    g2_sy_ring = ring("sy", sy, N_SY, lambda peer: g2_sy.at[sy], g2_sy, g2_sems.at[3])
-
-    g1_sy_ring.wait_recv()
-    sums = jnp.sum(g1_sy[...].astype(F32), axis=0) * (524288.0**-0.5)
-    g1_done[sx, af_x] = sums.astype(BF16)
+    sums = jnp.sum(g2_far[...].astype(F32), axis=0).astype(BF16)
+    both[sy, 1, :16] = sums[:, :128]
+    both[sy, 1, 16:] = sums[:, 128:]
+    g2_sy_group = Group(N_SY, lambda j: both.at[sy, 1], both.at[sy, 1], along_sy, g2_sems.at[4])
+    g1_sy_group.wait_recv()
+    sums = jnp.sum(both[:, 0].astype(F32), axis=0)
+    g1_done[sx, af_x] = (sums * 524288.0**-0.5).astype(BF16)
     g1_done_group = Group(
         16,
         lambda j: g1_done.at[sx, af_x],
         g1_done.at[sx, af_x],
         near_device,
-        g1_sems.at[3],
-    )
-
-    g2_sy_ring.wait_recv()
-    sums = jnp.sum(g2_sy[...].astype(F32), axis=0) * (1.0 / 256.0)
-    g2_done[sx] = sums.astype(BF16)
-    g2_done_ring = ring("sx", sx, N_SX, lambda peer: g2_done.at[sx], g2_done, g2_sems.at[4])
-
+        g1_sems.at[2],
+    )
+    g2_sy_group.wait_recv()
+    sums = jnp.sum(both[:, 1].astype(F32), axis=0)
+    g2_done[sx] = (sums * (1.0 / 256.0)).astype(BF16)
+    g2_done_ring = ring("sx", sx, N_SX, lambda peer: g2_done.at[sx], g2_done, g2_sems.at[3])
     g2_done_ring.wait_recv()
-    for k in range(27):
-        half, place = k // 14, k % 14
-        q = place // 4
-        tile = g2_done[q].astype(F32)[8 * half : 8 * half + 8]
-        grad_two_ref[k] = tile[:, 64 * (place % 4) : 64 * (place % 4) + 64]
-
+    two_ref[...] = g2_done[...]
     g1_done_group.wait_recv()
-    for t in range(7):
-        rows = [
-            g1_done[q, t // 2].astype(F32)[:, 128 * (t % 2) : 128 * (t % 2) + 128]
-            for q in range(4)
-        ]
-        tile = jnp.concatenate(rows, axis=0).T
-        for k in range(4 * t, min(4 * t + 4, 27)):
-            grad_one_ref[k] = tile[32 * (k - 4 * t) : 32 * (k - 4 * t) + 32]
+    one_ref[...] = g1_done[...].reshape(16, 32, 128)
 
     for wait in pending:
         wait()
 
 
+def unpack(output, one, two, output_ref, grad_one_ref, grad_two_ref):
+    output_ref[...] = output[...]
+    for k in range(27):
+        half = 64 * (k // 16)
+        grad_one_ref[k] = one[k % 16].astype(F32)[:, half : half + 64]
+        half, place = k // 14, k % 14
+        tile = two[place // 4].astype(F32)
+        row, column = 16 * (place % 4 // 2) + 8 * half, 64 * (place % 2)
+        grad_two_ref[k] = tile[row : row + 8, column : column + 64]
+
+
 def per_device(inputs, weight_one, weight_two, cotangent):
-    x = inputs.reshape(32, 2, 512).transpose(1, 0, 2)
+    x = inputs.reshape(32, 2, 512)
     cot = cotangent.reshape(128, 128)
     vmem = pl.BlockSpec(memory_space=pltpu.VMEM)
-    output, grad_one, grad_two = pl.pallas_call(
+    output, one, two = pl.pallas_call(
         kernel,
         out_shape=(
             jax.ShapeDtypeStruct((128, 128), BF16),
-            jax.ShapeDtypeStruct((27, 32, 64), F32),
-            jax.ShapeDtypeStruct((27, 8, 64), F32),
+            jax.ShapeDtypeStruct((16, 32, 128), BF16),
+            jax.ShapeDtypeStruct((4, 32, 128), BF16),
         ),
         in_specs=[vmem] * 4,
         out_specs=(vmem, vmem, vmem),
@@ -538,14 +534,12 @@
             pltpu.VMEM((2, 4, 4, 16, 256), BF16),
             pltpu.VMEM((4, 16, 256), BF16),
             pltpu.VMEM((4, 16, 256), BF16),
-            pltpu.VMEM((8, 16, 256), BF16),
-            pltpu.VMEM((4, 16, 256), BF16),
-            pltpu.VMEM((64, 1024), F32),
-            pltpu.VMEM((4, 4, 16, 256), BF16),
-            pltpu.VMEM((4, 4, 16, 256), BF16),
-            pltpu.VMEM((4, 16, 256), BF16),
-            pltpu.VMEM((8, 16, 256), BF16),
-            pltpu.VMEM((4, 4, 16, 256), BF16),
+            pltpu.VMEM((4, 32, 128), BF16),
+            pltpu.VMEM((4, 4, 32, 128), BF16),
+            pltpu.VMEM((4, 4, 32, 128), BF16),
+            pltpu.VMEM((4, 32, 128), BF16),
+            pltpu.VMEM((4, 4, 32, 128), BF16),
+            pltpu.VMEM((8, 2, 32, 128), BF16),
             pltpu.SemaphoreType.DMA((3, 2, 4)),
             pltpu.SemaphoreType.DMA((3, 2, 8)),
             pltpu.SemaphoreType.DMA((2, 2, 4)),
@@ -556,6 +550,17 @@
             collective_id=0, has_side_effects=True, vmem_limit_bytes=48 * 2**20
         ),
     )(x, weight_one.transpose(0, 2, 1), weight_two, cot)
+    output, grad_one, grad_two = pl.pallas_call(
+        unpack,
+        out_shape=(
+            jax.ShapeDtypeStruct((128, 128), BF16),
+            jax.ShapeDtypeStruct((27, 32, 64), F32),
+            jax.ShapeDtypeStruct((27, 8, 64), F32),
+        ),
+        in_specs=[vmem] * 3,
+        out_specs=(vmem, vmem, vmem),
+        compiler_params=pltpu.CompilerParams(vmem_limit_bytes=16 * 2**20),
+    )(output, one, two)
     return output.reshape(128, 1, 1, 1, 128), grad_one.transpose(0, 2, 1), grad_two
 
 

time: 67 us -> 67.1 us (level)
    pallas_call x0 -> x1, Pallas kernels: none -> 0.89 us  [per_device(): pl.pallas_call(unpack, out_shape=(jax.ShapeDtypeStruct((128, 128), BF16),...]
    unnamed x10 -> x8, local copies, waits for them, and re-layouts: 3.83 us -> 3.34 us
where the time goes in v4:
time: 67.1 us; the launch traced here: 66.8 us
  Pallas kernels  62.8 us (94%)
  local copies, waits for them, and re-layouts  3.34 us (5%)
    pallas_call x1, Pallas kernels, per_device(): pl.pallas_call(kernel, out_shape=(jax.ShapeDtypeStruct((128, 128), BF16),...  61.9 us
    unnamed x8, local copies, waits for them, and re-layouts  3.34 us

profile of v4, /device:TPU:1, one launch (start us, length us, event | category | flops | bytes accessed | tf_op | source)
XLA Modules:
  0.0 66.8 jit_solution(18172803006845504777)
XLA Ops:
  0.6 0.0 copy-start
  0.6 0.9 %copy-done = bf16[27,64,32]{1,2,0:T(8,128)(2,1)S(1)} copy-done((bf16[27,64,32]{1,2,0:T(8,128)(2,1)S(1)}, bf16[27,64,32]{1,2,0:T(8,128)(2,1)}, u32[]{:S(2)}) %copy-start) | copy-done | bytes 110616
  1.6 0.0 copy-start.1
  1.6 0.8 %copy-done.1 = bf16[32,2,1,1,512]{4,1,3,2,0:T(2,128)(2,1)S(1)} copy-done((bf16[32,2,1,1,512]{4,1,3,2,0:T(2,128)(2,1)S(1)}, bf16[32,2,1,1,512]{4,1,3,2,0:T(2,128)(2,1)}, u32[]{:S(2)}) %copy-start.1) | copy-done | bytes 65560
  2.4 0.0 copy-start.2
  2.4 0.8 %copy-done.2 = bf16[27,8,64]{2,1,0:T(8,128)(2,1)S(1)} copy-done((bf16[27,8,64]{2,1,0:T(8,128)(2,1)S(1)}, bf16[27,8,64]{2,1,0:T(8,128)(2,1)}, u32[]{:S(2)}) %copy-start.2) | copy-done | bytes 27672
  3.2 0.0 copy-start.3
  3.2 0.8 %copy-done.3 = bf16[128,1,1,1,128]{4,0,3,2,1:T(8,128)(2,1)S(1)} copy-done((bf16[128,1,1,1,128]{4,0,3,2,1:T(8,128)(2,1)S(1)}, bf16[128,1,1,1,128]{4,0,3,2,1:T(8,128)(2,1)}, u32[]{:S(2)}) %copy-start.3) | copy-done | bytes 32792
  4.0 61.9 %shard_map.67 = (bf16[128,128]{1,0:T(8,128)(2,1)S(1)}, bf16[16,32,128]{2,1,0:T(8,128)(2,1)S(1)}, bf16[4,32,128]{2,1,0:T(8,128)(2,1)S(1)}) custom-call(bf16[32,2,512]{2,1,0:T(2,128)(2,1)S(1)} %bitcast.6, bf16[27,32,64]{2,1,0:T(8,128)(2,1)S(1)} %bitcast.5, bf16[27,8,64]{2,1,0:T(8,128)(2,1)S(1)} %copy-done.2, bf16[128,128]{1,0:T(8,128)(2,1)S(1)} %bitcast.7), custom_call_target="tpu_custom_call" | custom-call | tf_op jit(solution)/shard_map/pallas_call | solution.py:498
  65.9 0.9 %shard_map.68 = (bf16[128,128]{1,0:T(8,128)(2,1)}, f32[27,32,64]{2,1,0:T(8,128)}, f32[27,8,64]{2,1,0:T(8,128)}) custom-call(bf16[128,128]{1,0:T(8,128)(2,1)S(1)} %get-tuple-element.9.output, bf16[16,32,128]{2,1,0:T(8,128)(2,1)S(1)} %get-tuple-element.10.one, bf16[4,32,128]{2,1,0:T(8,128)(2,1)S(1)} %get-tuple-element.11.two), custom_call_target="tpu_custom_call" | custom-call | tf_op jit(solution)/shard_map/pallas_call | solution.py:553
Async XLA Ops:
  0.6 0.9 %copy-start = (bf16[27,64,32]{1,2,0:T(8,128)(2,1)S(1)}, bf16[27,64,32]{1,2,0:T(8,128)(2,1)}, u32[]{:S(2)}) copy-start(bf16[27,64,32]{1,2,0:T(8,128)(2,1)} %param.5) | copy-start | bytes 331780
  1.6 0.8 %copy-start.1 = (bf16[32,2,1,1,512]{4,1,3,2,0:T(2,128)(2,1)S(1)}, bf16[32,2,1,1,512]{4,1,3,2,0:T(2,128)(2,1)}, u32[]{:S(2)}) copy-start(bf16[32,2,1,1,512]{4,1,3,2,0:T(2,128)(2,1)} %param.4) | copy-start | bytes 196612
  2.4 0.8 %copy-start.2 = (bf16[27,8,64]{2,1,0:T(8,128)(2,1)S(1)}, bf16[27,8,64]{2,1,0:T(8,128)(2,1)}, u32[]{:S(2)}) copy-start(bf16[27,8,64]{2,1,0:T(8,128)(2,1)} %w2_ref.1) | copy-start | bytes 82948
  3.2 0.8 %copy-start.3 = (bf16[128,1,1,1,128]{4,0,3,2,1:T(8,128)(2,1)S(1)}, bf16[128,1,1,1,128]{4,0,3,2,1:T(8,128)(2,1)}, u32[]{:S(2)}) copy-start(bf16[128,1,1,1,128]{4,0,3,2,1:T(8,128)(2,1)} %param.7) | copy-start | bytes 98308

commit v5 on v4

--- a/solution.py
+++ b/solution.py
@@ -121,17 +121,6 @@
     for device in greeted:
         pl.semaphore_signal(barrier, inc=1, device_id=device, device_id_type=MESH)
 
-    x_raw = x_ref[...].astype(F32)
-    x_all[1] = x_raw[:, 0].astype(BF16)
-    x_all[2] = x_raw[:, 1].astype(BF16)
-    for t in range(7):
-        rows = []
-        for half in range(2):
-            pair = []
-            for k in (14 * half + 2 * t, 14 * half + 2 * t + 1):
-                pair.append(w2_ref[k].astype(F32) if k < 27 else jnp.zeros((8, 64), F32))
-            rows.append(jnp.concatenate(pair, axis=1))
-        w2_own[:, 128 * t : 128 * t + 128] = jnp.concatenate(rows, axis=0).astype(BF16)
     pl.semaphore_wait(barrier, len(greeted))
 
     pending = []
@@ -243,8 +232,16 @@
         return dot(joined, extend[...]).astype(BF16)
 
     x_copies = exchange_planes(
-        [(-1, x_all.at[1], 3), (1, x_all.at[2], 0)], x_all, z_sems.at[0]
-    )
+        [(-1, x_ref.at[0], 3), (1, x_ref.at[1], 0)], x_all, z_sems.at[0]
+    )
+    for t in range(7):
+        rows = []
+        for half in range(2):
+            pair = []
+            for k in (14 * half + 2 * t, 14 * half + 2 * t + 1):
+                pair.append(w2_ref[k].astype(F32) if k < 27 else jnp.zeros((8, 64), F32))
+            rows.append(jnp.concatenate(pair, axis=1))
+        w2_own[:, 128 * t : 128 * t + 128] = jnp.concatenate(rows, axis=0).astype(BF16)
     w2_far = Group(
         4,
         lambda j: w2_own,
@@ -254,6 +251,8 @@
     )
     c_copies = exchange_borders(cot_ref, c_recv, plane_sems.at[2])
 
+    x_all[1] = x_ref[0]
+    x_all[2] = x_ref[1]
     w2_all[af_x, af_y] = w2_own[...]
     select_one[...] = border_selection_one()
     place_one[...] = column_placement_one()
@@ -371,6 +370,30 @@
             delta_two = jnp.where(own, delta, 0.0).astype(BF16)
         shift_plane(delta, patches_d, 1152 * z, 128)
 
+    pooled_grad = dot(w2_turned[...], patches_d[...]).astype(BF16)
+
+    spread = dot(pooled_grad, spread_select[...]) * 0.125
+    total = None
+    for z in range(2):
+        delta_one = (spread * slope(hidden_one[z])).T.astype(BF16)
+        part = dot(patches_one[288 * z : 288 * z + 864], delta_one)
+        total = part if total is None else total + part
+    rest = jnp.concatenate([total[512:], jnp.zeros((160, 64), F32)], axis=0)
+    sums = jnp.concatenate([total[:512], rest], axis=1).astype(BF16)
+    g1_send[...] = sums.reshape(4, 4, 32, 128)
+
+    def near(j):
+        return lax.rem(sx + j // 4, N_SX), lax.rem(af_x + j % 4, 4)
+
+    def near_device(j):
+        return {"sx": near(j)[0], "af": af_y * 4 + near(j)[1]}
+
+    def far_device(j):
+        return {"af": lax.rem(af_y + j, 4) * 4 + af_x}
+
+    g1_near = Group(16, lambda j: g1_send.at[near(j)], g1_recv.at[sx, af_x], near_device, g1_sems.at[0])
+    g1_recv[sx, af_x] = g1_send[sx, af_x]
+
     halves = []
     for half in range(2):
         start = 576 + 896 * half
@@ -389,30 +412,6 @@
         g2_sems.at[0],
     )
 
-    pooled_grad = dot(w2_turned[...], patches_d[...]).astype(BF16)
-
-    spread = dot(pooled_grad, spread_select[...]) * 0.125
-    total = None
-    for z in range(2):
-        delta_one = (spread * slope(hidden_one[z])).T.astype(BF16)
-        part = dot(patches_one[288 * z : 288 * z + 864], delta_one)
-        total = part if total is None else total + part
-    rest = jnp.concatenate([total[512:], jnp.zeros((160, 64), F32)], axis=0)
-    sums = jnp.concatenate([total[:512], rest], axis=1).astype(BF16)
-    g1_send[...] = sums.reshape(4, 4, 32, 128)
-
-    def near(j):
-        return lax.rem(sx + j // 4, N_SX), lax.rem(af_x + j % 4, 4)
-
-    def near_device(j):
-        return {"sx": near(j)[0], "af": af_y * 4 + near(j)[1]}
-
-    def far_device(j):
-        return {"af": lax.rem(af_y + j, 4) * 4 + af_x}
-
-    g1_near = Group(16, lambda j: g1_send.at[near(j)], g1_recv.at[sx, af_x], near_device, g1_sems.at[0])
-    g1_recv[sx, af_x] = g1_send[sx, af_x]
-
     g2_core.wait_recv()
     mine = g2_send[core].astype(F32) + g2_pair[...].astype(F32)
     g2_part[...] = mine.astype(BF16)
@@ -492,7 +491,7 @@
 
 
 def per_device(inputs, weight_one, weight_two, cotangent):
-    x = inputs.reshape(32, 2, 512)
+    x = inputs.reshape(32, 2, 512).transpose(1, 0, 2)
     cot = cotangent.reshape(128, 128)
     vmem = pl.BlockSpec(memory_space=pltpu.VMEM)
     output, one, two = pl.pallas_call(

time: 67.1 us -> 65.1 us (0.970)
  local copies, waits for them, and re-layouts: 3.34 us -> 1.81 us
    unnamed x8 -> x7, local copies, waits for them, and re-layouts: 3.34 us -> 1.81 us
where the time goes in v5:
time: 65.1 us; the launch traced here: 64.9 us
  Pallas kernels  62.4 us (96%)
  local copies, waits for them, and re-layouts  1.81 us (3%)
  between operations  0.68 us (1%)
    pallas_call x1, Pallas kernels, per_device(): pl.pallas_call(kernel, out_shape=(jax.ShapeDtypeStruct((128, 128), BF16),...  61.5 us
    unnamed x7, local copies, waits for them, and re-layouts  1.81 us

profile of v5, /device:TPU:1, one launch (start us, length us, event | category | flops | bytes accessed | tf_op | source)
XLA Modules:
  0.0 64.9 jit_solution(6442362912110151788)
XLA Ops:
  0.6 0.0 copy-start.1
  0.6 0.0 copy-start.2
  0.7 0.9 %copy.9 = bf16[32,2,1,1,512]{4,0,1,3,2:T(8,128)(2,1)S(1)} copy(bf16[32,2,1,1,512]{4,1,3,2,0:T(2,128)(2,1)} %param.4) | data formatting | bytes 131072 | tf_op args[0]
  1.5 0.0 copy-done.1
  1.5 0.0 copy-done.2
  1.5 0.0 copy-start
  1.6 0.9 %copy-done = bf16[27,64,32]{1,2,0:T(8,128)(2,1)S(1)} copy-done((bf16[27,64,32]{1,2,0:T(8,128)(2,1)S(1)}, bf16[27,64,32]{1,2,0:T(8,128)(2,1)}, u32[]{:S(2)}) %copy-start) | copy-done | bytes 110616
  2.5 61.5 %shard_map.67 = (bf16[128,128]{1,0:T(8,128)(2,1)S(1)}, bf16[16,32,128]{2,1,0:T(8,128)(2,1)S(1)}, bf16[4,32,128]{2,1,0:T(8,128)(2,1)S(1)}) custom-call(bf16[2,32,512]{2,1,0:T(8,128)(2,1)S(1)} %bitcast.9, bf16[27,32,64]{2,1,0:T(8,128)(2,1)S(1)} %bitcast.10, bf16[27,8,64]{2,1,0:T(8,128)(2,1)S(1)} %copy-done.1, bf16[128,128]{1,0:T(8,128)(2,1)S(1)} %bitcast.11), custom_call_target="tpu_custom_call" | custom-call | tf_op jit(solution)/shard_map/pallas_call | solution.py:497
  64.0 0.9 %shard_map.68 = (bf16[128,128]{1,0:T(8,128)(2,1)}, f32[27,32,64]{2,1,0:T(8,128)}, f32[27,8,64]{2,1,0:T(8,128)}) custom-call(bf16[128,128]{1,0:T(8,128)(2,1)S(1)} %get-tuple-element.9.output, bf16[16,32,128]{2,1,0:T(8,128)(2,1)S(1)} %get-tuple-element.10.one, bf16[4,32,128]{2,1,0:T(8,128)(2,1)S(1)} %get-tuple-element.11.two), custom_call_target="tpu_custom_call" | custom-call | tf_op jit(solution)/shard_map/pallas_call | solution.py:552
Async XLA Ops:
  0.6 0.9 %copy-start.1 = (bf16[27,8,64]{2,1,0:T(8,128)(2,1)S(1)}, bf16[27,8,64]{2,1,0:T(8,128)(2,1)}, u32[]{:S(2)}) copy-start(bf16[27,8,64]{2,1,0:T(8,128)(2,1)} %w2_ref.1) | copy-start | bytes 82948
  0.6 0.9 %copy-start.2 = (bf16[128,1,1,1,128]{4,0,3,2,1:T(8,128)(2,1)S(1)}, bf16[128,1,1,1,128]{4,0,3,2,1:T(8,128)(2,1)}, u32[]{:S(2)}) copy-start(bf16[128,1,1,1,128]{4,0,3,2,1:T(8,128)(2,1)} %param.7) | copy-start | bytes 98308
  1.5 0.9 %copy-start = (bf16[27,64,32]{1,2,0:T(8,128)(2,1)S(1)}, bf16[27,64,32]{1,2,0:T(8,128)(2,1)}, u32[]{:S(2)}) copy-start(bf16[27,64,32]{1,2,0:T(8,128)(2,1)} %param.5) | copy-start | bytes 331780

commit v6 on v5

--- a/solution.py
+++ b/solution.py
@@ -115,7 +115,7 @@
         if dx or dy
     ]
     greeted += [{"af": lax.rem(af + step, N_AF)} for step in (1, N_AF - 1)]
-    greeted += [{"af": af_y * 4 + lax.rem(af_x + j, 4)} for j in (1, 2, 3)]
+    greeted += [{"af": af_y * 4 + lax.rem(af_x + j, 4)} for j in (1, 3)]
     greeted += [{"af": lax.rem(af_y + j, 4) * 4 + af_x} for j in (1, 2, 3)]
     greeted += [{"sy": lax.rem(sy + N_SY // 2, N_SY)}]
     for device in greeted:
@@ -249,7 +249,6 @@
         lambda j: {"af": lax.rem(af_y + j, 4) * 4 + af_x},
         w2_sems.at[0],
     )
-    c_copies = exchange_borders(cot_ref, c_recv, plane_sems.at[2])
 
     x_all[1] = x_ref[0]
     x_all[2] = x_ref[1]
@@ -262,6 +261,7 @@
     spread_select[...] = spread_selection()
     interior_select[...] = interior_selection()
     patches_two[2880:2944] = jnp.zeros((64, 256), BF16)
+    c_copies = exchange_borders(cot_ref, c_recv, plane_sems.at[2])
     for copy in x_copies:
         copy.wait_recv()
 

time: 65.1 us -> 65.1 us (level)
  no operation moved by 1% of the time
where the time goes in v6:
time: 65.1 us; the launch traced here: 64.9 us
  Pallas kernels  62.4 us (96%)
  local copies, waits for them, and re-layouts  1.81 us (3%)
  between operations  0.68 us (1%)
    pallas_call x1, Pallas kernels, per_device(): pl.pallas_call(kernel, out_shape=(jax.ShapeDtypeStruct((128, 128), BF16),...  61.5 us
    unnamed x7, local copies, waits for them, and re-layouts  1.81 us

profile of v6, /device:TPU:1, one launch (start us, length us, event | category | flops | bytes accessed | tf_op | source)
XLA Modules:
  0.0 64.9 jit_solution(14080430427757372630)
XLA Ops:
  0.6 0.0 copy-start.1
  0.6 0.0 copy-start.2
  0.7 0.9 %copy.9 = bf16[32,2,1,1,512]{4,0,1,3,2:T(8,128)(2,1)S(1)} copy(bf16[32,2,1,1,512]{4,1,3,2,0:T(2,128)(2,1)} %param.4) | data formatting | bytes 131072 | tf_op args[0]
  1.5 0.0 copy-done.1
  1.5 0.0 copy-done.2
  1.5 0.0 copy-start
  1.6 0.9 %copy-done = bf16[27,64,32]{1,2,0:T(8,128)(2,1)S(1)} copy-done((bf16[27,64,32]{1,2,0:T(8,128)(2,1)S(1)}, bf16[27,64,32]{1,2,0:T(8,128)(2,1)}, u32[]{:S(2)}) %copy-start) | copy-done | bytes 110616
  2.5 61.5 %shard_map.67 = (bf16[128,128]{1,0:T(8,128)(2,1)S(1)}, bf16[16,32,128]{2,1,0:T(8,128)(2,1)S(1)}, bf16[4,32,128]{2,1,0:T(8,128)(2,1)S(1)}) custom-call(bf16[2,32,512]{2,1,0:T(8,128)(2,1)S(1)} %bitcast.9, bf16[27,32,64]{2,1,0:T(8,128)(2,1)S(1)} %bitcast.10, bf16[27,8,64]{2,1,0:T(8,128)(2,1)S(1)} %copy-done.1, bf16[128,128]{1,0:T(8,128)(2,1)S(1)} %bitcast.11), custom_call_target="tpu_custom_call" | custom-call | tf_op jit(solution)/shard_map/pallas_call | solution.py:497
  64.0 0.9 %shard_map.68 = (bf16[128,128]{1,0:T(8,128)(2,1)}, f32[27,32,64]{2,1,0:T(8,128)}, f32[27,8,64]{2,1,0:T(8,128)}) custom-call(bf16[128,128]{1,0:T(8,128)(2,1)S(1)} %get-tuple-element.9.output, bf16[16,32,128]{2,1,0:T(8,128)(2,1)S(1)} %get-tuple-element.10.one, bf16[4,32,128]{2,1,0:T(8,128)(2,1)S(1)} %get-tuple-element.11.two), custom_call_target="tpu_custom_call" | custom-call | tf_op jit(solution)/shard_map/pallas_call | solution.py:552
Async XLA Ops:
  0.6 0.9 %copy-start.1 = (bf16[27,8,64]{2,1,0:T(8,128)(2,1)S(1)}, bf16[27,8,64]{2,1,0:T(8,128)(2,1)}, u32[]{:S(2)}) copy-start(bf16[27,8,64]{2,1,0:T(8,128)(2,1)} %w2_ref.1) | copy-start | bytes 82948
  0.6 0.9 %copy-start.2 = (bf16[128,1,1,1,128]{4,0,3,2,1:T(8,128)(2,1)S(1)}, bf16[128,1,1,1,128]{4,0,3,2,1:T(8,128)(2,1)}, u32[]{:S(2)}) copy-start(bf16[128,1,1,1,128]{4,0,3,2,1:T(8,128)(2,1)} %param.7) | copy-start | bytes 98308
  1.5 0.9 %copy-start = (bf16[27,64,32]{1,2,0:T(8,128)(2,1)S(1)}, bf16[27,64,32]{1,2,0:T(8,128)(2,1)}, u32[]{:S(2)}) copy-start(bf16[27,64,32]{1,2,0:T(8,128)(2,1)} %param.5) | copy-start | bytes 331780
